TPU v7x, 32 devices: a whole 2x2x4 slice. The times are simulated.
32 devices in a mesh: dp: 8 (over z, x), chan: 4 (over y, core).
Axes of the slice: x: 2, y: 2, z: 4, core: 2. Of those that a mesh axis runs over, the one named last changes fastest.
Arguments:
- images: bfloat16 [640, 9, 9, 512], P('dp'), may hold values from -6 to 6
- groups: int32 [640], P('dp'), may hold values from 0 to 2
- cotangent: bfloat16 [640, 9, 9, 512], P('dp', None, None, 'chan'), may hold values from -6 to 6
- weight_one: float32 [9, 512, 512], P(None, None, 'chan'), may hold values from -0.09375 to 0.09375
- gain_one: float32 [512], P('chan'), may hold values from 0.5 to 1.5
- shift_one: float32 [512], P('chan'), may hold values from -3 to 3
- weight_two: float32 [9, 512, 512], P(None, None, 'chan'), may hold values from -0.09375 to 0.09375
- gain_two: float32 [512], P('chan'), may hold values from 0.5 to 1.5
- shift_two: float32 [512], P('chan'), may hold values from -3 to 3
- moment_one: float32 [9, 512, 512], P(None, None, 'chan'), may hold values from -0.0006 to 0.0006
- moment_two: float32 [9, 512, 512], P(None, None, 'chan'), may hold values from -0.0006 to 0.0006
Outputs:
- block_output: bfloat16 [640, 9, 9, 512], P('dp', None, None, 'chan')
- input_grad: float32 [640, 9, 9, 512], P('dp', None, None, 'chan')
- weight_one_grad: float32 [9, 512, 512], P(None, None, 'chan')
- gain_one_grad: float32 [512], P('chan')
- shift_one_grad: float32 [512], P('chan')
- weight_two_grad: float32 [9, 512, 512], P(None, None, 'chan')
- gain_two_grad: float32 [512], P('chan')
- shift_two_grad: float32 [512], P('chan')
- moment_one_new: float32 [9, 512, 512], P(None, None, 'chan')
- moment_two_new: float32 [9, 512, 512], P(None, None, 'chan')
- weight_norms: float32 [2], replicated
- grad_norms: float32 [2], replicated
All inputs are finite; a program needn't handle non-finite values.
Results may differ from a plain program's by a relative error of at most 0.015.
Values may be sent and summed in bfloat16 or wider, within the bound.
No kernel may reach another device: no remote copies, remote signals or barrier semaphores. Data moves between devices by JAX's collectives and lax.ppermute only.
A program may use at most 256 MiB of HBM per device.

v0:
```python
import jax
import jax.numpy as jnp
from jax import lax
from jax.sharding import PartitionSpec as P

EPSILON = 1e-05
MOMENTUM = 0.9
LEARN_RATE = 8.0
TRUST_COEF = 0.001
DECAY = 5e-05


def valid_pixels(groups, side):
    extent = 5 + 2 * groups
    places = jnp.arange(side, dtype=jnp.int32)
    inside = (places[None, :, None] < extent[:, None, None]) & (
        places[None, None, :] < extent[:, None, None]
    )
    return inside.astype(jnp.float32)[..., None]


def conv_forward(gathered, kernel):
    side = gathered.shape[1]
    padded = jnp.pad(gathered, ((0, 0), (1, 1), (1, 1), (0, 0)))
    total = jnp.zeros(gathered.shape[:3] + (kernel.shape[2],), jnp.float32)
    for i in range(3):
        for j in range(3):
            total = total + jnp.einsum(
                "bhwc,cd->bhwd",
                padded[:, i : i + side, j : j + side, :],
                kernel[3 * i + j],
                preferred_element_type=jnp.float32,
            )
    return total


def conv_back_data(grad_low, kernel):
    side = grad_low.shape[1]
    padded = jnp.pad(grad_low, ((0, 0), (1, 1), (1, 1), (0, 0)))
    total = jnp.zeros(grad_low.shape[:3] + (kernel.shape[1],), jnp.float32)
    for i in range(3):
        for j in range(3):
            total = total + jnp.einsum(
                "bhwd,cd->bhwc",
                padded[:, 2 - i : 2 - i + side, 2 - j : 2 - j + side, :],
                kernel[3 * i + j],
                preferred_element_type=jnp.float32,
            )
    return total


def kernel_grad(gathered, grad_low):
    side = gathered.shape[1]
    padded = jnp.pad(gathered, ((0, 0), (1, 1), (1, 1), (0, 0)))
    pieces = []
    for i in range(3):
        for j in range(3):
            pieces.append(
                jnp.einsum(
                    "bhwc,bhwd->cd",
                    padded[:, i : i + side, j : j + side, :],
                    grad_low,
                    preferred_element_type=jnp.float32,
                )
            )
    return jnp.stack(pieces)


def moments(hidden, valid_mask, local_count):
    first, pixel_count = lax.psum((jnp.sum(hidden * valid_mask, axis=(0, 1, 2)), local_count), "dp")
    center = first / pixel_count
    centered = hidden - center
    second = lax.psum(jnp.sum(valid_mask * centered * centered, axis=(0, 1, 2)), "dp")
    spread = second / pixel_count
    return (center, spread, pixel_count)


def layer_forward(gathered, kernel_low, gain, shift, valid_mask, local_count):
    hidden = conv_forward(gathered, kernel_low)
    center, spread, pixel_count = moments(hidden, valid_mask, local_count)
    rscale = lax.rsqrt(spread + EPSILON)
    normed = (hidden - center) * rscale
    return (normed, rscale, pixel_count, normed * gain + shift)


def layer_backward(grad_z, normed, rscale, pixel_count, gain, gathered, kernel_low, valid_mask):
    gain_grad, shift_grad = lax.psum(
        (jnp.sum(grad_z * normed, axis=(0, 1, 2)), jnp.sum(grad_z, axis=(0, 1, 2))), "dp"
    )
    grad_h = (
        gain
        * rscale
        * (grad_z - shift_grad / pixel_count - normed * gain_grad / pixel_count)
        * valid_mask
    ).astype(jnp.bfloat16)
    weight_grad = lax.psum(kernel_grad(gathered, grad_h), "dp")
    partial_sums = conv_back_data(grad_h, kernel_low)
    grad_act = lax.psum_scatter(
        partial_sums.astype(jnp.bfloat16), "chan", scatter_dimension=3, tiled=True
    ).astype(jnp.float32)
    return (gain_grad, shift_grad, weight_grad, grad_act)


def gelu_grad(point, incoming):
    return jax.vjp(jax.nn.gelu, point)[1](incoming)[0]


def shards(
    images,
    groups,
    cotangent,
    weight_one,
    gain_one,
    shift_one,
    weight_two,
    gain_two,
    shift_two,
    moment_one,
    moment_two,
):
    valid_mask = valid_pixels(groups, images.shape[1])
    local_count = jnp.sum(valid_mask)
    width = weight_one.shape[2]
    start = lax.axis_index("chan") * width
    masked_full = (images.astype(jnp.float32) * valid_mask).astype(jnp.bfloat16)
    masked_in = lax.dynamic_slice_in_dim(masked_full, start, width, 3)
    kernel_one = weight_one.astype(jnp.bfloat16)
    kernel_two = weight_two.astype(jnp.bfloat16)
    normed_one, rscale_one, pixel_count, z_one = layer_forward(
        masked_full, kernel_one, gain_one, shift_one, valid_mask, local_count
    )
    active = (jax.nn.gelu(z_one) * valid_mask).astype(jnp.bfloat16)
    gathered_two = lax.all_gather(active, "chan", axis=3, tiled=True)
    normed_two, rscale_two, pixel_count, z_two = layer_forward(
        gathered_two, kernel_two, gain_two, shift_two, valid_mask, local_count
    )
    pre_act = z_two + masked_in.astype(jnp.float32)
    block_output = (jax.nn.gelu(pre_act) * valid_mask).astype(jnp.bfloat16)
    grad_pre = gelu_grad(pre_act, cotangent.astype(jnp.float32) * valid_mask)
    gain_two_grad, shift_two_grad, weight_two_grad, grad_active = layer_backward(
        grad_pre,
        normed_two,
        rscale_two,
        pixel_count,
        gain_two,
        gathered_two,
        kernel_two,
        valid_mask,
    )
    grad_z_one = gelu_grad(z_one, grad_active * valid_mask)
    gain_one_grad, shift_one_grad, weight_one_grad, grad_conv_in = layer_backward(
        grad_z_one,
        normed_one,
        rscale_one,
        pixel_count,
        gain_one,
        masked_full,
        kernel_one,
        valid_mask,
    )
    input_grad = (grad_pre + grad_conv_in) * valid_mask
    local_squares = jnp.stack(
        [
            jnp.stack(
                [jnp.sum(weight_one * weight_one), jnp.sum(weight_one_grad * weight_one_grad)]
            ),
            jnp.stack(
                [jnp.sum(weight_two * weight_two), jnp.sum(weight_two_grad * weight_two_grad)]
            ),
        ]
    )
    all_norms = jnp.sqrt(lax.psum(local_squares, "chan"))
    weight_norms = all_norms[:, 0]
    grad_norms = all_norms[:, 1]
    trust_one = TRUST_COEF * weight_norms[0] / (grad_norms[0] + DECAY * weight_norms[0])
    trust_two = TRUST_COEF * weight_norms[1] / (grad_norms[1] + DECAY * weight_norms[1])
    moment_one_new = MOMENTUM * moment_one + LEARN_RATE * trust_one * (
        weight_one_grad + DECAY * weight_one
    )
    moment_two_new = MOMENTUM * moment_two + LEARN_RATE * trust_two * (
        weight_two_grad + DECAY * weight_two
    )
    return (
        block_output,
        input_grad,
        weight_one_grad,
        gain_one_grad,
        shift_one_grad,
        weight_two_grad,
        gain_two_grad,
        shift_two_grad,
        moment_one_new,
        moment_two_new,
        weight_norms,
        grad_norms,
    )


def solution(mesh):
    placed = (
        P("dp", None, None, None),
        P("dp"),
        P("dp", None, None, "chan"),
        P(None, None, "chan"),
        P("chan"),
        P("chan"),
        P(None, None, "chan"),
        P("chan"),
        P("chan"),
        P(None, None, "chan"),
        P(None, None, "chan"),
    )
    return jax.shard_map(
        shards,
        mesh=mesh,
        in_specs=placed,
        out_specs=(
            P("dp", None, None, "chan"),
            P("dp", None, None, "chan"),
            P(None, None, "chan"),
            P("chan"),
            P("chan"),
            P(None, None, "chan"),
            P("chan"),
            P("chan"),
            P(None, None, "chan"),
            P(None, None, "chan"),
            P(),
            P(),
        ),
        check_vma=False,
    )
```

profile of v0, /device:TPU:0, one launch (start us, length us, event | category | flops | bytes accessed | tf_op | source)
XLA Modules:
  0.0 821.0 jit_solution(11432110465632400960)
XLA Ops:
  12.1 4.8 multiply_convert_fusion
  42.8 8.5 %multiply_reduce_fusion.3 = (f32[128]{0:T(128)S(1)}, f32[80,9,9,128]{3,0,2,1:T(8,128)S(1)}) fusion(f32[80,9,9]{0,2,1:T(8,128)S(1)} %and_convert_fusion, bf16[80,9,9,512]{3,0,2,1:T(8,128)(2,1)S(1)} %multiply_convert_fusion, bf16[9,512,128]{2,1,0:T(8,128)(2,1)} %copy-done.10, f32[80,9,9,128]{3,0,2,1:T(8,128)S(1)} %fusion.47, ...), kind=kOutput, calls=%fused_computation.34 | convolution fusion | flops 679382912 | bytes 36652864 | tf_op jit(solution)/shard_map/bhwc,cd->bhwd/dot_general | solution.py:28
  51.3 23.8 %all-reduce.6 = (f32[128]{0:T(128)S(1)}, f32[]{:T(128)}) all-reduce(f32[128]{0:T(128)S(1)} %get-tuple-element.41, f32[]{:T(128)} %convert_reduce_fusion), channel_id=1, replica_groups=mesh['dp'=8,'chan'=4] {'dp'}, use_global_device_ids=true, to_apply=%region_1.2 | all-reduce | flops 129 | bytes 1032 | tf_op jit(solution)/shard_map/psum | solution.py:70
  76.8 17.1 %psum.89 = f32[128]{0:T(128)S(1)} all-reduce(f32[128]{0:T(128)S(1)} %fusion.12), channel_id=1, replica_groups=mesh['dp'=8,'chan'=4] {'dp'}, use_global_device_ids=true, to_apply=%region_5.6 | all-reduce | flops 128 | bytes 1024 | tf_op jit(solution)/shard_map/psum | solution.py:73
  102.0 44.5 %all-gather.2.cloned.1.call-done = bf16[80,9,9,512]{3,0,2,1:T(8,128)(2,1)} async-done(((bf16[80,9,9,128]{3,0,2,1:T(8,128)(2,1)}), bf16[80,9,9,512]{3,0,2,1:T(8,128)(2,1)}) %all-gather.2.cloned.1.call-update) | async-done | bytes 6635536 | tf_op jit(solution)/shard_map/all_gather | solution.py:133
  146.5 4.7 fusion.63
  175.0 8.4 %multiply_reduce_fusion.2 = (f32[128]{0:T(128)S(1)}, f32[80,9,9,128]{3,0,2,1:T(8,128)S(1)}) fusion(f32[80,9,9]{0,2,1:T(8,128)S(1)} %and_convert_fusion, bf16[80,9,9,512]{3,0,2,1:T(8,128)(2,1)S(1)} %copy-done.1, bf16[9,512,128]{2,1,0:T(8,128)(2,1)} %copy-done.12, f32[80,9,9,128]{3,0,2,1:T(8,128)S(1)} %fusion.63, f32[80,9,9,128]{3,0,2,1:T(8,128)S(1)} %fusion.61, ...), kind=kOutput, calls=%fused_computation.30 | convolution fusion | flops 679382912 | bytes 36652864 | tf_op jit(solution)/shard_map/bhwc,cd->bhwd/dot_general | solution.py:28
  183.5 21.5 %psum.90 = f32[128]{0:T(128)S(1)} all-reduce(f32[128]{0:T(128)S(1)} %get-tuple-element.43), channel_id=1, replica_groups=mesh['dp'=8,'chan'=4] {'dp'}, use_global_device_ids=true, to_apply=%region_7.8 | all-reduce | flops 128 | bytes 1024 | tf_op jit(solution)/shard_map/psum | solution.py:70
  206.7 17.1 %psum.91 = f32[128]{0:T(128)S(1)} all-reduce(f32[128]{0:T(128)S(1)} %fusion.13), channel_id=1, replica_groups=mesh['dp'=8,'chan'=4] {'dp'}, use_global_device_ids=true, to_apply=%region_9.10 | all-reduce | flops 128 | bytes 1024 | tf_op jit(solution)/shard_map/psum | solution.py:73
  224.5 6.8 fusion.65
  231.2 19.1 %all-reduce.5 = (f32[128]{0:T(128)S(1)}, f32[128]{0:T(128)S(1)}) all-reduce(f32[128]{0:T(128)S(1)} %get-tuple-element.15, f32[128]{0:T(128)S(1)} %get-tuple-element.14), channel_id=1, replica_groups=mesh['dp'=8,'chan'=4] {'dp'}, use_global_device_ids=true, to_apply=%region_13.14 | all-reduce | flops 256 | bytes 2048 | tf_op jit(solution)/shard_map/psum | solution.py:87
  251.0 4.7 multiply_convert_fusion.2
  255.8 6.6 fusion.62
  262.4 6.7 fusion.60
  269.1 6.6 fusion.58
  275.7 6.6 fusion.54
  282.3 6.6 fusion.52
  288.8 6.6 fusion.50
  295.4 6.8 fusion.48
  302.2 6.7 fusion.56
  308.9 36.4 %add_convert_fusion.1 = bf16[80,9,9,512]{3,0,2,1:T(8,128)(2,1)} fusion(f32[80,9,9,512]{3,0,2,1:T(8,128)} %fusion.62, f32[80,9,9,512]{3,0,2,1:T(8,128)} %fusion.60, f32[80,9,9,512]{3,0,2,1:T(8,128)} %fusion.58, f32[80,9,9,512]{3,0,2,1:T(8,128)} %fusion.56, f32[80,9,9,512]{3,0,2,1:T(8,128)} %fusion.54, f32[80,9,9,512]{3,0,2,1:T(8,128)} %fusion.52, ...), kind=kOutput, calls=%fused_computation.1 | convolution fusion | flops 700948480 | bytes 114593792 | tf_op jit(solution)/shard_map/bhwd,cd->bhwc/dot_general | solution.py:43
  345.3 21.4 %copy.66 = bf16[80,9,9,512]{0,2,1,3:T(8,128)(2,1)} copy(bf16[80,9,9,512]{3,0,2,1:T(8,128)(2,1)} %add_convert_fusion.1) | data formatting | bytes 13271040
  366.8 21.4 %reshape.149 = bf16[512,6480]{1,0:T(8,128)(2,1)} reshape(bf16[512,9,9,80]{3,2,1,0:T(8,128)(2,1)} %bitcast.384) | data formatting | bytes 13271040
  388.3 5.9 fusion.21
  394.2 6.1 fusion.20
  400.3 5.3 fusion.19
  421.9 23.9 %reduce-scatter.7.cloned.1.call-done = bf16[128,6480]{1,0:T(8,128)(2,1)} async-done(((bf16[512,6480]{1,0:T(8,128)(2,1)}), bf16[128,6480]{1,0:T(8,128)(2,1)}) %reduce-scatter.7.cloned.1.call-update) | async-done | bytes 1658896
  445.8 7.2 reshape.150
  453.0 6.5 copy.67
  459.5 6.5 fusion.64
  466.0 21.3 %all-reduce.4 = (f32[128]{0:T(128)S(1)}, f32[128]{0:T(128)S(1)}) all-reduce(f32[128]{0:T(128)S(1)} %get-tuple-element.13, f32[128]{0:T(128)S(1)} %get-tuple-element.12), channel_id=1, replica_groups=mesh['dp'=8,'chan'=4] {'dp'}, use_global_device_ids=true, to_apply=%region_18.19 | all-reduce | flops 256 | bytes 2048 | tf_op jit(solution)/shard_map/psum | solution.py:87
  495.4 6.6 fusion.46
  502.1 6.7 fusion.44
  508.7 6.6 fusion.42
  515.3 6.7 fusion.38
  522.0 6.6 fusion.36
  528.6 6.8 fusion.34
  535.5 6.6 fusion.32
  565.3 7.6 fusion.40
  572.9 36.6 %add_convert_fusion = bf16[80,9,9,512]{3,0,2,1:T(8,128)(2,1)} fusion(f32[80,9,9,512]{3,0,2,1:T(8,128)} %fusion.46, f32[80,9,9,512]{3,0,2,1:T(8,128)} %fusion.44, f32[80,9,9,512]{3,0,2,1:T(8,128)} %fusion.42, f32[80,9,9,512]{3,0,2,1:T(8,128)} %fusion.40, f32[80,9,9,512]{3,0,2,1:T(8,128)} %fusion.38, f32[80,9,9,512]{3,0,2,1:T(8,128)} %fusion.36, ...), kind=kOutput, calls=%fused_computation | convolution fusion | flops 700948480 | bytes 114593792 | tf_op jit(solution)/shard_map/bhwd,cd->bhwc/dot_general | solution.py:43
  609.5 21.4 %copy.68 = bf16[80,9,9,512]{0,2,1,3:T(8,128)(2,1)} copy(bf16[80,9,9,512]{3,0,2,1:T(8,128)(2,1)} %add_convert_fusion) | data formatting | bytes 13271040
  630.9 21.5 %reshape.151 = bf16[512,6480]{1,0:T(8,128)(2,1)} reshape(bf16[512,9,9,80]{3,2,1,0:T(8,128)(2,1)} %bitcast.385) | data formatting | bytes 13271040
  652.5 77.9 %all-reduce.10.cloned.1.call-done = (f32[9,512,128]{2,1,0:T(8,128)}, f32[9,512,128]{2,1,0:T(8,128)}) async-done(((f32[9,512,128]{2,1,0:T(8,128)}, f32[9,512,128]{2,1,0:T(8,128)}), (f32[9,512,128]{2,1,0:T(8,128)}, f32[9,512,128]{2,1,0:T(8,128)})) %all-reduce.10.cloned.1.call-update) | async-done | bytes 4718608 | tf_op jit(solution)/shard_map/psum | solution.py:96
  738.9 7.0 psum.98
  751.2 8.9 %multiply_add_fusion.1 = (f32[9,512,128]{2,1,0:T(8,128)}, f32[9,512,128]{2,1,0:T(8,128)}) fusion(f32[9,512,128]{2,1,0:T(8,128)S(1)} %copy-done.7, f32[9,512,128]{2,1,0:T(8,128)} %param.17, f32[9,512,128]{2,1,0:T(8,128)} %param.21, f32[]{:T(128)} %bitcast.151, f32[9,512,128]{2,1,0:T(8,128)} %get-tuple-element.49, f32[9,512,128]{2,1,0:T(8,128)} %param.14, ...), kind=kLoop, calls=%fused_computation.38 | loop fusion | flops 5898240 | bytes 18874376 | tf_op jit(solution)/shard_map/add | solution.py:180
  760.1 32.9 %reduce-scatter.9.cloned.1.call-done = bf16[128,6480]{1,0:T(8,128)(2,1)} async-done(((bf16[512,6480]{1,0:T(8,128)(2,1)}), bf16[128,6480]{1,0:T(8,128)(2,1)}) %reduce-scatter.9.cloned.1.call-update) | async-done | bytes 1658896
  793.0 7.2 reshape.152
  800.2 6.6 copy.69
  (133 shorter events, 132.6 us)
Async XLA Ops:
  7.2 139.3 %all-gather.2.cloned.1.call-start = ((), (), s32[]{:S(2)}) async-start(), calls=%async_computation.2 | async-start | bytes 8294400 | tf_op jit(solution)/shard_map/all_gather | solution.py:133
  12.1 27.1 %copy-start.10 = (bf16[9,512,128]{2,1,0:T(8,128)(2,1)}, bf16[9,512,128]{2,1,0:T(8,128)(2,1)S(1)}, u32[]{:S(2)}) copy-start(bf16[9,512,128]{2,1,0:T(8,128)(2,1)S(1)} %get-tuple-element.34) | copy-start | bytes 3538948
  16.9 25.9 %copy-start = (bf16[80,9,9,512]{3,0,2,1:T(8,128)(2,1)}, bf16[80,9,9,512]{3,0,2,1:T(8,128)(2,1)S(1)}, u32[]{:S(2)}) copy-start(bf16[80,9,9,512]{3,0,2,1:T(8,128)(2,1)S(1)} %multiply_convert_fusion) | copy-start | bytes 19906564
  51.3 47.0 %copy-start.4 = (f32[80,9,9,128]{3,0,2,1:T(8,128)}, f32[80,9,9,128]{3,0,2,1:T(8,128)S(1)}, u32[]{:S(2)}) copy-start(f32[80,9,9,128]{3,0,2,1:T(8,128)S(1)} %get-tuple-element.42) | copy-start | bytes 9953284
  51.3 42.6 %copy-start.18 = (f32[128]{0:T(128)S(1)}, f32[128]{0:T(128)}, u32[]{:S(2)}) copy-start(f32[128]{0:T(128)} %param.15) | copy-start | bytes 1540
  51.3 44.3 %copy-start.22 = (f32[128]{0:T(128)S(1)}, f32[128]{0:T(128)}, u32[]{:S(2)}) copy-start(f32[128]{0:T(128)} %param.16) | copy-start | bytes 1540
  75.7 22.6 %copy-start.14 = (f32[128]{0:T(128)}, f32[128]{0:T(128)S(1)}, u32[]{:S(2)}) copy-start(f32[128]{0:T(128)S(1)} %broadcast_divide_fusion.3) | copy-start | bytes 1540
  95.1 0.5 copy-start.16
  98.4 347.4 %reduce-scatter.7.cloned.1.call-start = ((), (), s32[]{:S(2)}) async-start(), calls=%async_computation.3 | async-start | bytes 8355840
  102.0 69.4 %copy-start.12 = (bf16[9,512,128]{2,1,0:T(8,128)(2,1)}, bf16[9,512,128]{2,1,0:T(8,128)(2,1)S(1)}, u32[]{:S(2)}) copy-start(bf16[9,512,128]{2,1,0:T(8,128)(2,1)S(1)} %get-tuple-element.36) | copy-start | bytes 3538948
  146.5 4.7 copy-start.1
  183.4 47.8 %copy-start.5 = (f32[80,9,9,128]{3,0,2,1:T(8,128)}, f32[80,9,9,128]{3,0,2,1:T(8,128)S(1)}, u32[]{:S(2)}) copy-start(f32[80,9,9,128]{3,0,2,1:T(8,128)S(1)} %get-tuple-element.44) | copy-start | bytes 9953284
  183.5 40.3 %copy-start.20 = (f32[128]{0:T(128)S(1)}, f32[128]{0:T(128)}, u32[]{:S(2)}) copy-start(f32[128]{0:T(128)} %param.18) | copy-start | bytes 1540
  183.5 41.0 %copy-start.24 = (f32[128]{0:T(128)S(1)}, f32[128]{0:T(128)}, u32[]{:S(2)}) copy-start(f32[128]{0:T(128)} %param.19) | copy-start | bytes 1540
  250.4 5.4 copy-start.25
  250.4 5.4 copy-start.27
  251.0 4.8 copy-start.13
  388.2 342.2 %all-reduce.10.cloned.1.call-start = ((), (), s32[]{:S(2)}) async-start(), calls=%async_computation.5 | async-start | bytes 9437184 | tf_op jit(solution)/shard_map/psum | solution.py:96
  394.2 11.4 %slice-start.2 = ((s8[6635520]{0:T(1024)(128)(4,1)}), s8[4194304]{0:T(1024)(128)(4,1)S(1)}, s32[]{:S(2)}) async-start(s8[6635520]{0:T(1024)(128)(4,1)} %bitcast.382), calls=%async_computation.8 | async-start | bytes 8388608
  400.3 5.3 slice-start.3
  453.0 6.5 copy-start.15
  453.0 6.5 copy-start.17
  453.0 6.5 copy-start.19
  453.0 6.5 copy-start.23
  459.5 28.7 %copy-start.21 = (f32[128]{0:T(128)S(1)}, f32[128]{0:T(128)}, u32[]{:S(2)}) copy-start(f32[128]{0:T(128)} %get-tuple-element.26) | copy-start | bytes 1540
  459.5 33.2 %slice-start = ((s8[6635520]{0:T(1024)(128)(4,1)}), s8[2441216]{0:T(1024)(128)(4,1)S(1)}, s32[]{:S(2)}) async-start(s8[6635520]{0:T(1024)(128)(4,1)} %bitcast.380), calls=%async_computation.6 | async-start | bytes 4882432
  487.3 5.4 copy-start.26
  487.3 5.4 copy-start.28
  487.3 5.4 slice-start.1
  492.8 68.4 %copy-start.2 = (bf16[80,9,9,128]{3,0,2,1:T(8,128)(2,1)}, bf16[80,9,9,128]{3,0,2,1:T(8,128)(2,1)S(1)}, u32[]{:S(2)}) copy-start(bf16[80,9,9,128]{3,0,2,1:T(8,128)(2,1)S(1)} %multiply_convert_fusion.1) | copy-start | bytes 4976644
  492.8 2.7 copy-start.11
  563.9 1.4 copy-start.3
  563.9 229.1 %reduce-scatter.9.cloned.1.call-start = ((), (), s32[]{:S(2)}) async-start(), calls=%async_computation.4 | async-start | bytes 8355840
  730.4 20.8 %copy-start.7 = (f32[9,512,128]{2,1,0:T(8,128)S(1)}, f32[9,512,128]{2,1,0:T(8,128)}, u32[]{:S(2)}) copy-start(f32[9,512,128]{2,1,0:T(8,128)} %get-tuple-element.52) | copy-start | bytes 7077892
  800.2 6.6 copy-start.6
  806.8 3.6 copy-start.9
  810.3 2.5 copy-start.8
Sparse Core Ops, SparseCore 0:
  98.5 47.9 all-gather.1
  388.3 57.4 reduce-scatter.6
  564.0 166.3 all-reduce.9
  733.0 59.9 reduce-scatter.8
where the time goes:
time: 833 us; the launch traced here: 821 us
  matrix products  310 us (37%)
  waiting for transfers between devices  179 us (21%)
  blocking collectives  127 us (15%)
  local copies, waits for them, and re-layouts  120 us (14%)
  other arithmetic  66.2 us (8%)
  between operations  18.3 us (2%)
    dot_general x18, matrix products, conv_back_data(): jnp.einsum('bhwd,cd->bhwc', padded[:, 2 - i:2 - i + side, 2 - j:2 - j + s...  180 us
    unnamed x76, local copies, waits for them, and re-layouts  119 us
    psum x1, waiting for transfers between devices, layer_backward(): weight_grad = lax.psum(kernel_grad(gathered, grad_h), 'dp')  77.9 us
    dot_general x18, matrix products, conv_forward(): jnp.einsum('bhwc,cd->bhwd', padded[:, i:i + side, j:j + side, :], kernel[...  71.3 us
    dot_general x18, matrix products, kernel_grad(): jnp.einsum('bhwc,bhwd->cd', padded[:, i:i + side, j:j + side, :], grad_lo...  58.2 us
    unnamed x6, waiting for transfers between devices  56.8 us
    psum x2, blocking collectives, moments(): lax.psum((jnp.sum(hidden * valid_mask, axis=(0, 1, 2)), local_count), 'dp')  45.2 us
    all_gather x1, waiting for transfers between devices, shards(): gathered_two = lax.all_gather(active, 'chan', axis=3, tiled=True)  44.5 us
  transfers between devices with their start and end apart: 4, of which 4 were waited for; matrix products, arithmetic and copies ran while one was open for 17% of the time, Pallas kernels for 0%

commit v1 on v0

v1 whole, which is shorter than its diff:
```python
import functools

import jax
import jax.numpy as jnp
from jax import lax
from jax.experimental import pallas as pl
from jax.experimental.pallas import tpu as pltpu
from jax.sharding import PartitionSpec as P

EPSILON = 1e-05
MOMENTUM = 0.9
LEARN_RATE = 8.0
TRUST_COEF = 0.001
DECAY = 5e-05
GELU_A = 0.7978845608028654
GELU_B = 0.7978845608028654 * 0.044715
F32 = jnp.float32
BF16 = jnp.bfloat16
LANES = 128
PAIRS = ((0, 2), (2, 4), (4, 6), (6, 8), (8, 9))
VMEM_BYTES = 56 * 1024 * 1024


def chunk_starts(side, sizes):
    starts, at = [], 0
    for size in sizes:
        starts.append(at)
        at += size
    assert at == side
    return starts


def segments(*splits):
    ends = sorted({sum(s[: k + 1]) for s in splits for k in range(len(s))})
    result, start = [], 0
    for end in ends:
        where = []
        for s in splits:
            at = 0
            for index, size in enumerate(s):
                if at <= start < at + size:
                    where.append((index, at))
                at += size
        result.append((start, end, where))
        start = end
    return result


def pixel_mask(ext, r, c):
    return jnp.where(ext > jnp.maximum(r, c), 1.0, 0.0).astype(F32)


def gelu(v):
    t = jnp.tanh(v * (GELU_A + GELU_B * (v * v)))
    half = 0.5 * v
    return half + half * t


def gelu_both(v):
    sq = v * v
    t = jnp.tanh(v * (GELU_A + GELU_B * sq))
    half = 0.5 * v
    value = half + half * t
    slope = 0.5 + 0.5 * t + (half - half * (t * t)) * (GELU_A + (3.0 * GELU_B) * sq)
    return value, slope


def call(body, outs, ins, scratch=(), flops=0, bytes_=0, aliases=None, any_in=(), any_out=(), smem_in=()):
    vm = pl.BlockSpec(memory_space=pltpu.VMEM)
    anys = pl.BlockSpec(memory_space=pl.ANY)
    sm = pl.BlockSpec(memory_space=pltpu.SMEM)
    in_specs = [anys if k in any_in else sm if k in smem_in else vm for k in range(len(ins))]
    out_specs = [anys if k in any_out else vm for k in range(len(outs))]
    return pl.pallas_call(
        body,
        out_shape=[jax.ShapeDtypeStruct(s, d) for s, d in outs],
        in_specs=in_specs,
        out_specs=out_specs,
        scratch_shapes=list(scratch),
        input_output_aliases=aliases or {},
        compiler_params=pltpu.CompilerParams(vmem_limit_bytes=VMEM_BYTES),
        cost_estimate=pl.CostEstimate(flops=int(flops), bytes_accessed=int(bytes_), transcendentals=0),
    )(*ins)


def prep_body(xor_rows, chan_ref, w_ref, wb_ref, wt_ref, sq_ref):
    chan = chan_ref[0]
    blocks = wt_ref.shape[0]
    total = jnp.zeros((8, LANES), F32)
    for k in range(blocks):
        other = jnp.bitwise_xor(chan, k)
        rows = pl.ds(pl.multiple_of(other * LANES, LANES), LANES)
        for t in range(9):
            piece = w_ref[t, rows, :]
            total = total + jnp.sum((piece * piece).reshape(LANES // 8, 8, LANES), axis=0)
            low = piece.astype(BF16)
            if xor_rows:
                wb_ref[k * LANES : (k + 1) * LANES, t * LANES : (t + 1) * LANES] = low
            else:
                wb_ref[rows, t * LANES : (t + 1) * LANES] = low
            wt_ref[k, :, (8 - t) * LANES : (9 - t) * LANES] = piece.T.astype(BF16)
    sq_ref[...] = total


def prep(weight, chan, xor_rows):
    width = weight.shape[1]
    blocks = width // LANES
    return call(
        functools.partial(prep_body, xor_rows),
        [((width, 9 * LANES), BF16), ((blocks, LANES, 9 * LANES), BF16), ((8, LANES), F32)],
        [chan, weight],
        smem_in=(0,),
        bytes_=weight.size * 8,
    )


def add_row(lhs, w_ref, acc, slot, batch):
    rows = lhs.shape[0]
    for a, b in PAIRS:
        y = jnp.dot(lhs, w_ref[:, a * LANES : b * LANES], preferred_element_type=F32)
        for t in range(a, b):
            i, j = divmod(t, 3)
            z = y[:, (t - a) * LANES : (t - a + 1) * LANES]
            at = slot + 2 - i
            if j == 0:
                acc[at, batch:] += z[: rows - batch]
            elif j == 1:
                acc[at] += z
            else:
                acc[at, : rows - batch] += z[batch:]


def start_acc(acc, carry_ref):
    for slot in range(acc.shape[0]):
        if carry_ref is not None and slot < 2:
            acc[slot] = carry_ref[slot]
        else:
            acc[slot] = jnp.zeros(acc.shape[1:], F32)


def emitted(r0, count, side):
    first = 0 if r0 == 0 else r0 - 1
    last = side if r0 + count == side else r0 + count - 1
    return first, last, first - (r0 - 1)


def chunk_stats(acc, slot0, first, count, ext, side, batch, prev_ref, mean_only_ref=None):
    zero = jnp.zeros((batch, LANES), F32)

    def sums(k, carry):
        s, n = carry
        for c in range(side):
            m = pixel_mask(ext, first + k, c)
            s = s + m * acc[slot0 + k, c * batch : (c + 1) * batch, :]
            n = n + m
        return s, n

    s, n = lax.fori_loop(0, count, sums, (zero, zero))
    s = jnp.sum(s, axis=0, keepdims=True)
    n = jnp.sum(n, axis=0, keepdims=True)
    return s / jnp.maximum(n, 1.0), n


def merge_rows(mean_a, m2_a, n_a, mean_b, m2_b, n_b):
    n = n_a + n_b
    safe = jnp.maximum(n, 1.0)
    delta = mean_a - mean_b
    mean = (n_a * mean_a + n_b * mean_b) / safe
    return mean, m2_a + m2_b + delta * delta * (n_a * n_b / safe), n


def conv_forward_body(kind, r0, count, side, batch, blocks, *refs):
    refs = list(refs)
    ext_ref = refs.pop(0)
    w_ref = refs.pop(0)
    if kind == "images":
        sources = [refs.pop(0)]
        affine_ref = None
    else:
        sources = [refs.pop(0) for _ in range(blocks)]
        affine_ref = refs.pop(0)
    carry_ref = prev_ref = None
    if r0:
        carry_ref, prev_ref = refs.pop(0), refs.pop(0)
    h_ref, stat_ref = refs.pop(0), refs.pop(0)
    low_ref = refs.pop(0) if kind == "images" else None
    act_ref = refs.pop(0) if kind != "images" else None
    last_chunk = r0 + count == side
    carry_out = None if last_chunk else refs.pop(0)
    acc, row = refs[0], refs[1] if kind == "images" else None
    sem = refs[2] if kind == "images" else None
    width = blocks * LANES
    ext = ext_ref[...]
    start_acc(acc, carry_ref)

    if kind == "images":
        x_hbm = sources[0]

        def fetch(t, slot):
            return pltpu.make_async_copy(x_hbm.at[r0 + t], row.at[slot], sem.at[slot])

        fetch(0, 0).start()

        @pl.loop(0, count)
        def _(t):
            slot = lax.rem(t, 2)

            @pl.when(t + 1 < count)
            def _():
                fetch(t + 1, 1 - slot).start()

            fetch(t, slot).wait()
            pieces = []
            for c in range(side):
                m = pixel_mask(ext, r0 + t, c).astype(BF16)
                x = row[slot, c]
                pieces.append(
                    jnp.concatenate([x[:, k * LANES : (k + 1) * LANES] * m for k in range(blocks)], axis=1)
                )
            add_row(jnp.concatenate(pieces, axis=0), w_ref, acc, t, batch)
    else:

        @pl.loop(0, count)
        def _(t):
            for k in range(blocks):
                scale = affine_ref[k, 0:1, :]
                shift = affine_ref[k, 1:2, :]
                for c in range(side):
                    m = pixel_mask(ext, r0 + t, c)
                    z = sources[k][t, c].astype(F32) * scale + shift
                    act_ref[t, c, :, k * LANES : (k + 1) * LANES] = (gelu(z) * m).astype(BF16)
            add_row(act_ref[t].reshape(side * batch, width), w_ref, acc, t, batch)

    first, last, slot0 = emitted(r0, count, side)
    rows = last - first
    mean, n = chunk_stats(acc, slot0, first, rows, ext, side, batch, prev_ref)

    def squares(k, total):
        for c in range(side):
            m = pixel_mask(ext, first + k, c)
            h = acc[slot0 + k, c * batch : (c + 1) * batch, :]
            d = h - mean
            h_ref[k, c] = h
            if low_ref is not None:
                low_ref[k, c] = d.astype(BF16)
            total = total + m * (d * d)
        return total

    m2 = lax.fori_loop(0, rows, squares, jnp.zeros((batch, LANES), F32))
    m2 = jnp.sum(m2, axis=0, keepdims=True)
    whole = (mean, m2, n)
    if prev_ref is not None:
        whole = merge_rows(mean, m2, n, prev_ref[0:1], prev_ref[1:2], prev_ref[2:3])
    stat_ref[0:1] = whole[0]
    stat_ref[1:2] = whole[1]
    stat_ref[2:3] = whole[2]
    stat_ref[3:4] = mean
    stat_ref[4:8] = jnp.zeros((4, LANES), F32)
    if carry_out is not None:
        carry_out[0] = acc[count]
        carry_out[1] = acc[count + 1]


def conv_forward(kind, r0, count, ext, weights, sources, affine, carry, prev):
    side, batch = sources[0].shape[1], sources[0].shape[2]
    width = weights.shape[0]
    blocks = width // LANES
    first, last, _ = emitted(r0, count, side)
    rows = last - first
    ins = [ext, weights] + list(sources)
    if kind != "images":
        ins.append(affine)
    if r0:
        ins += [carry, prev]
    outs = [((rows, side, batch, LANES), F32), ((8, LANES), F32)]
    scratch = [pltpu.VMEM((count + 2, side * batch, LANES), F32)]
    any_in = ()
    if kind == "images":
        outs.append(((rows, side, batch, LANES), BF16))
        scratch += [pltpu.VMEM((2, side, batch, width), BF16), pltpu.SemaphoreType.DMA((2,))]
        any_in = (2,)
    else:
        outs.append(((count, side, batch, width), BF16))
    if r0 + count != side:
        outs.append(((2, side * batch, LANES), F32))
    return call(
        functools.partial(conv_forward_body, kind, r0, count, side, batch, blocks),
        outs,
        ins,
        scratch,
        flops=2 * count * side * batch * width * 9 * LANES,
        bytes_=count * side * batch * width * 2,
        any_in=any_in,
    )


def conv_back_body(kind, r0, count, side, batch, blocks, h_split, *refs):
    refs = list(refs)
    ext_ref, w_ref = refs.pop(0), refs.pop(0)
    sources = [refs.pop(0) for _ in range(blocks)]
    carry_ref = refs.pop(0) if r0 else None
    first, last, slot0 = emitted(r0, count, side)
    rows = last - first
    if kind == "active":
        affine_ref = refs.pop(0)
        prev_ref = refs.pop(0) if r0 else None
        parts = [s for s in segments(h_split) if s[1] > first and s[0] < last]
        h_refs = {s[2][0][0]: refs.pop(0) for s in parts}
        out_ref, sum_ref = refs.pop(0), refs.pop(0)
    else:
        grad_ref = refs.pop(0)
        if r0:
            refs.pop(0)
        out_hbm = refs.pop(0)
    carry_out = None if r0 + count == side else refs.pop(0)
    acc, lhs_ref = refs.pop(0), refs.pop(0)
    ext = ext_ref[...]
    start_acc(acc, carry_ref)

    @pl.loop(0, count)
    def _(t):
        lhs = jnp.concatenate([sources[k][t].reshape(side * batch, LANES) for k in range(blocks)], axis=1)
        add_row(lhs, w_ref, acc, t, batch)

    if carry_out is not None:
        carry_out[0] = acc[count]
        carry_out[1] = acc[count + 1]
    if kind == "active":
        scale, shift = affine_ref[0:1, :], affine_ref[1:2, :]
        rscale, offset = affine_ref[2:3, :], affine_ref[3:4, :]
        zero = jnp.zeros((batch, LANES), F32)
        total = (zero, zero)
        for start, stop, where in parts:
            index, base = where[0]
            lo, hi = max(start, first), min(stop, last)

            def one(r, carry, index=index, base=base):
                ds, dn = carry
                for c in range(side):
                    m = pixel_mask(ext, r, c)
                    h = h_refs[index][r - base, c]
                    _, slope = gelu_both(h * scale + shift)
                    dz = acc[slot0 + r - first, c * batch : (c + 1) * batch, :] * m * slope
                    out_ref[r - first, c] = dz
                    ds = ds + dz
                    dn = dn + dz * (h * rscale + offset)
                return ds, dn

            total = lax.fori_loop(lo, hi, one, total)
        ds = jnp.sum(total[0], axis=0, keepdims=True)
        dn = jnp.sum(total[1], axis=0, keepdims=True)
        if prev_ref is not None:
            ds = ds + prev_ref[0:1]
            dn = dn + prev_ref[1:2]
        sum_ref[0:1] = ds
        sum_ref[1:2] = dn
        sum_ref[2:8] = jnp.zeros((6, LANES), F32)
    else:
        stage, sem = refs.pop(0), refs.pop(0)

        @pl.loop(0, rows)
        def _(k):
            for c in range(side):
                m = pixel_mask(ext, first + k, c)
                stage[k, c] = m * (grad_ref[k, c] + acc[slot0 + k, c * batch : (c + 1) * batch, :])
            pltpu.make_async_copy(stage.at[k], out_hbm.at[first + k], sem.at[k]).start()

        @pl.loop(0, rows)
        def _(k):
            pltpu.make_async_copy(stage.at[k], out_hbm.at[first + k], sem.at[k]).wait()


def conv_back(kind, r0, count, ext, weights, sources, carry, extra, h_split=None, prev=None, target=None):
    side, batch = sources[0].shape[1], sources[0].shape[2]
    blocks = len(sources)
    first, last, _ = emitted(r0, count, side)
    rows = last - first
    ins = [ext, weights] + list(sources)
    if r0:
        ins.append(carry)
    scratch = [pltpu.VMEM((count + 2, side * batch, LANES), F32), pltpu.VMEM((8, LANES), F32)]
    aliases, any_in, any_out = {}, (), ()
    if kind == "active":
        affine, h_parts = extra
        ins.append(affine)
        if r0:
            ins.append(prev)
        for s in segments(h_split):
            if s[1] > first and s[0] < last:
                ins.append(h_parts[s[2][0][0]])
        outs = [((rows, side, batch, LANES), F32), ((8, LANES), F32)]
    else:
        ins.append(extra)
        if r0:
            any_in = (len(ins),)
            aliases = {len(ins): 0}
            ins.append(target)
        outs = [((side, side, batch, LANES), F32)]
        any_out = (0,)
        scratch += [pltpu.VMEM((rows, side, batch, LANES), F32), pltpu.SemaphoreType.DMA((rows,))]
    if r0 + count != side:
        outs.append(((2, side * batch, LANES), F32))
    return call(
        functools.partial(conv_back_body, kind, r0, count, side, batch, blocks, h_split),
        outs,
        ins,
        scratch,
        flops=2 * count * side * batch * blocks * LANES * 9 * LANES,
        bytes_=count * side * batch * blocks * LANES * 2,
        aliases=aliases,
        any_in=any_in,
        any_out=any_out,
    )


def weight_grad_body(kind, side, batch, blocks, splits, *refs):
    refs = list(refs)
    chan_ref = refs.pop(0)
    ext_ref = refs.pop(0)
    x_refs = [refs.pop(0) for _ in splits[0]]
    g_refs = [refs.pop(0) for _ in splits[1]]
    out_ref, acc, gs = refs
    chan = chan_ref[0]
    ext = ext_ref[...]
    rows = side * batch
    gs[0] = jnp.zeros((rows, LANES), BF16)
    gs[side + 1] = jnp.zeros((rows, LANES), BF16)
    at = 0
    for ref, size in zip(g_refs, splits[1]):
        for k in range(size):
            gs[at + k + 1] = ref[k].reshape(rows, LANES)
        at += size
    acc[...] = jnp.zeros(acc.shape, F32)
    edge = jnp.zeros((batch, LANES), BF16)
    at = 0
    for ref, size in zip(x_refs, splits[0]):

        @pl.loop(at, at + size)
        def _(r, ref=ref, at=at):
            if kind == "images":
                pieces = []
                for c in range(side):
                    m = pixel_mask(ext, r, c).astype(BF16)
                    x = ref[r - at, c]
                    pieces.append(
                        jnp.concatenate([x[:, k * LANES : (k + 1) * LANES] * m for k in range(blocks)], axis=1)
                    )
                x = jnp.concatenate(pieces, axis=0)
            else:
                x = ref[r - at].reshape(rows, blocks * LANES)
            parts = []
            for i in range(3):
                g = gs[r + 2 - i]
                parts.append(jnp.concatenate([g[batch:], edge], axis=0))
                parts.append(g)
                parts.append(jnp.concatenate([edge, g[: rows - batch]], axis=0))
            wide = jnp.concatenate(parts, axis=1)
            acc[...] += lax.dot_general(
                x, wide, (((0,), (0,)), ((), ())), preferred_element_type=F32
            )

        at += size
    for k in range(blocks):
        if kind == "images":
            rows_out = pl.ds(k * LANES, LANES)
        else:
            rows_out = pl.ds(pl.multiple_of(jnp.bitwise_xor(chan, k) * LANES, LANES), LANES)
        for t in range(9):
            out_ref[t, rows_out, :] = acc[k * LANES : (k + 1) * LANES, t * LANES : (t + 1) * LANES]


def weight_grad(kind, chan, ext, xs, gs):
    side, batch, width = xs[0].shape[1], xs[0].shape[2], xs[0].shape[3]
    blocks = width // LANES
    splits = ([x.shape[0] for x in xs], [g.shape[0] for g in gs])
    return call(
        functools.partial(weight_grad_body, kind, side, batch, blocks, splits),
        [((9, width, LANES), F32)],
        [chan, ext] + list(xs) + list(gs),
        [pltpu.VMEM((width, 9 * LANES), F32), pltpu.VMEM((side + 2, side * batch, LANES), BF16)],
        flops=2 * side * side * batch * width * 9 * LANES,
        bytes_=side * side * batch * width * 2,
        smem_in=(0,),
    )[0]


def block_end_body(side, batch, h_split, out_split, *refs):
    refs = list(refs)
    chan_ref, ext_ref, affine_ref, images_hbm, cot_ref = refs[:5]
    refs = refs[5:]
    h_refs = [refs.pop(0) for _ in h_split]
    out_ref = refs.pop(0)
    grad_refs = [refs.pop(0) for _ in out_split]
    sum_ref, own, sem = refs
    lanes = pl.ds(pl.multiple_of(chan_ref[0] * LANES, LANES), LANES)
    copy = pltpu.make_async_copy(images_hbm.at[:, :, :, lanes], own, sem)
    copy.start()
    copy.wait()
    ext = ext_ref[...]
    scale, shift = affine_ref[0:1, :], affine_ref[1:2, :]
    rscale, offset = affine_ref[2:3, :], affine_ref[3:4, :]
    zero = jnp.zeros((batch, LANES), F32)
    total = (zero, zero)
    for start, stop, ((hi, hb), (gi, gb)) in segments(h_split, out_split):

        def one(r, carry, hi=hi, hb=hb, gi=gi, gb=gb):
            ds, dn = carry
            for c in range(side):
                m = pixel_mask(ext, r, c)
                h = h_refs[hi][r - hb, c]
                pre = h * scale + shift + own[r, c].astype(F32) * m
                value, slope = gelu_both(pre)
                out_ref[r, c] = (value * m).astype(BF16)
                dz = cot_ref[r, c].astype(F32) * m * slope
                grad_refs[gi][r - gb, c] = dz
                ds = ds + dz
                dn = dn + dz * (h * rscale + offset)
            return ds, dn

        total = lax.fori_loop(start, stop, one, total)
    sum_ref[0:1] = jnp.sum(total[0], axis=0, keepdims=True)
    sum_ref[1:2] = jnp.sum(total[1], axis=0, keepdims=True)
    sum_ref[2:8] = jnp.zeros((6, LANES), F32)


def block_end(chan, ext, affine, images, cotangent, h_parts, out_split):
    side, batch = images.shape[1], images.shape[2]
    h_split = [h.shape[0] for h in h_parts]
    outs = [((side, side, batch, LANES), BF16)]
    outs += [((n, side, batch, LANES), F32) for n in out_split]
    outs.append(((8, LANES), F32))
    return call(
        functools.partial(block_end_body, side, batch, h_split, out_split),
        outs,
        [chan, ext, affine, images, cotangent] + list(h_parts),
        [pltpu.VMEM((side, side, batch, LANES), BF16), pltpu.SemaphoreType.DMA],
        flops=side * side * batch * LANES * 100,
        bytes_=side * side * batch * LANES * 20,
        smem_in=(0,),
        any_in=(3,),
    )


def norm_back_body(side, batch, splits, *refs):
    refs = list(refs)
    ext_ref, coef_ref = refs.pop(0), refs.pop(0)
    h_refs = [refs.pop(0) for _ in splits[0]]
    dz_refs = [refs.pop(0) for _ in splits[1]]
    out_refs = [refs.pop(0) for _ in splits[2]]
    ext = ext_ref[...]
    a, b, c0 = coef_ref[0:1, :], coef_ref[1:2, :], coef_ref[2:3, :]
    for start, stop, ((hi, hb), (zi, zb), (oi, ob)) in segments(*splits):

        @pl.loop(start, stop)
        def _(r, hi=hi, hb=hb, zi=zi, zb=zb, oi=oi, ob=ob):
            for c in range(side):
                m = pixel_mask(ext, r, c)
                grad = a * dz_refs[zi][r - zb, c] - (h_refs[hi][r - hb, c] * b + c0)
                out_refs[oi][r - ob, c] = (m * grad).astype(BF16)


def norm_back(ext, coef, h_parts, dz_parts, out_split):
    side, batch = h_parts[0].shape[1], h_parts[0].shape[2]
    splits = ([h.shape[0] for h in h_parts], [z.shape[0] for z in dz_parts], list(out_split))
    return call(
        functools.partial(norm_back_body, side, batch, splits),
        [((n, side, batch, LANES), BF16) for n in out_split],
        [ext, coef] + list(h_parts) + list(dz_parts),
        flops=side * side * batch * LANES * 8,
        bytes_=side * side * batch * LANES * 10,
    )


def swap(x, axis, size, k):
    return lax.ppermute(x, axis, [(i, i ^ k) for i in range(size)])


def sum_over(x, axis, size):
    k = 1
    while k < size:
        x = x + swap(x, axis, size, k)
        k *= 2
    return x


def merge_over(stats, axis, size):
    k = 1
    while k < size:
        other = swap(stats, axis, size, k)
        stats = jnp.stack(merge_rows(stats[0], stats[1], stats[2], other[0], other[1], other[2]))
        k *= 2
    return stats


def gather_blocks(x, size):
    far = swap(x, "chan", size, 2)
    near = swap(x, "chan", size, 1)
    return [x, near, far, swap(far, "chan", size, 1)]


def reduce_grad(grad, size):
    index = lax.axis_index("dp")
    current = grad.reshape(-1, LANES)
    k = 1
    while k < size:
        half = current.shape[0] // 2
        low, high = current[:half], current[half:]
        upper = (index // k) % 2 == 1
        keep = jnp.where(upper, high, low)
        send = jnp.where(upper, low, high).astype(BF16)
        current = keep + swap(send, "dp", size, k).astype(F32)
        k *= 2
    squares = jnp.sum(current * current)
    current = current.astype(BF16)
    while k > 1:
        k //= 2
        other = swap(current, "dp", size, k)
        upper = (index // k) % 2 == 1
        current = jnp.where(upper, jnp.concatenate([other, current]), jnp.concatenate([current, other]))
    return current.astype(F32).reshape(grad.shape), squares


def layer_affine(stats, gain, shift):
    center, spread = stats[0], stats[1] / stats[2]
    rscale = lax.rsqrt(spread + EPSILON)
    scale = rscale * gain
    return jnp.stack([scale, shift - center * scale, rscale, -center * rscale])


def back_coef(affine, sums, count):
    scale, rscale, offset = affine[0], affine[2], affine[3]
    shift_grad, gain_grad = sums[0] / count, sums[1] / count
    return jnp.stack([scale, scale * rscale * gain_grad, scale * (shift_grad + offset * gain_grad)])


def shards(
    dp, ch, images, groups, cotangent, weight_one, gain_one, shift_one, weight_two, gain_two, shift_two, moment_one, moment_two
):
    side = images.shape[1]
    images = jnp.transpose(images, (1, 2, 0, 3))
    cotangent = jnp.transpose(cotangent, (1, 2, 0, 3))
    batch = images.shape[2]
    chan = lax.axis_index("chan").astype(jnp.int32).reshape(1)
    ext = jnp.broadcast_to((5 + 2 * groups)[:, None], (batch, LANES))
    third = side // 3
    conv_in = (third + 1, third, side - 2 * third - 1)
    flow = (third, third, side - 2 * third)
    flow_out = (third - 1, third, side - 2 * third + 1)

    wb_one, wt_one, sq_one = prep(weight_one, chan, False)
    wb_two, wt_two, sq_two = prep(weight_two, chan, True)

    h_one, low_one, means, carry, stat = [], [], [], None, None
    for r0, count in zip(chunk_starts(side, conv_in), conv_in):
        out = conv_forward("images", r0, count, ext, wb_one, [images], None, carry, stat)
        h, stat, low = out[:3]
        carry = out[3] if len(out) > 3 else None
        h_one.append(h)
        low_one.append(gather_blocks(low, ch))
        means.append(stat[3])
    stats_one = merge_over(stat[:3], "dp", dp)
    affine_one = layer_affine(stats_one, gain_one, shift_one)
    count_all = stats_one[2]
    params = jnp.stack([affine_one[0]] + [m * affine_one[0] + affine_one[1] for m in means])
    near = swap(params, "chan", ch, 1)
    both = jnp.stack([params, near])
    both = jnp.concatenate([both, swap(both, "chan", ch, 2)])

    h_two, act, carry, stat = [], [], None, None
    for q, (r0, count) in enumerate(zip(chunk_starts(side, flow), flow)):
        affine = jnp.stack([both[:, 0], both[:, 1 + q]], axis=1)
        out = conv_forward("blocks", r0, count, ext, wb_two, low_one[q], affine, carry, stat)
        h, stat, a = out[:3]
        carry = out[3] if len(out) > 3 else None
        h_two.append(h)
        act.append(a)
    stats_two = merge_over(stat[:3], "dp", dp)
    affine_two = layer_affine(stats_two, gain_two, shift_two)

    wt = jnp.stack([wt_one, wt_two], axis=1)
    wt, _ = lax.optimization_barrier((wt, stat))
    wt = [wt[0]] + [swap(wt[k], "chan", ch, k) for k in range(1, ch)]
    wt_one = jnp.concatenate([w[0] for w in wt])
    wt_two = jnp.concatenate([w[1] for w in wt])

    out = block_end(chan, ext, affine_two, images, cotangent, h_two, flow_out)
    block_output, grad_pre, sums = out[0], out[1:-1], out[-1]
    sums_two = sum_over(sums[:2], "dp", dp)
    grad_two = norm_back(ext, back_coef(affine_two, sums_two, count_all), h_two, grad_pre, flow)
    gathered = [gather_blocks(g, ch) for g in grad_two]
    weight_two_grad = weight_grad("act", chan, ext, act, grad_two)
    dz_one, carry, sums = [], None, None
    for q, (r0, count) in enumerate(zip(chunk_starts(side, flow), flow)):
        out = conv_back(
            "active", r0, count, ext, wt_two, gathered[q], carry, (affine_one, h_one), flow, sums
        )
        dz, sums = out[:2]
        carry = out[2] if len(out) > 2 else None
        dz_one.append(dz)
    sums_one = sum_over(sums[:2], "dp", dp)
    grad_one = norm_back(ext, back_coef(affine_one, sums_one, count_all), h_one, dz_one, flow)
    gathered = [gather_blocks(g, ch) for g in grad_one]
    weight_one_grad = weight_grad("images", chan, ext, [images], grad_one)
    input_grad, carry = None, None
    for q, (r0, count) in enumerate(zip(chunk_starts(side, flow), flow)):
        out = conv_back(
            "input", r0, count, ext, wt_one, gathered[q], carry, grad_pre[q], target=input_grad
        )
        input_grad = out[0]
        carry = out[1] if len(out) > 1 else None

    weight_two_grad, square_two = reduce_grad(weight_two_grad, dp)
    weight_one_grad, square_one = reduce_grad(weight_one_grad, dp)
    own = jnp.stack([jnp.sum(sq_one) / dp, jnp.sum(sq_two) / dp, square_one, square_two])
    norms = jnp.sqrt(sum_over(sum_over(own, "dp", dp), "chan", ch))
    weight_norms, grad_norms = norms[:2], norms[2:]
    trust = TRUST_COEF * weight_norms / (grad_norms + DECAY * weight_norms)
    moment_one_new = MOMENTUM * moment_one + LEARN_RATE * trust[0] * (weight_one_grad + DECAY * weight_one)
    moment_two_new = MOMENTUM * moment_two + LEARN_RATE * trust[1] * (weight_two_grad + DECAY * weight_two)
    return (
        jnp.transpose(block_output, (2, 0, 1, 3)),
        jnp.transpose(input_grad, (2, 0, 1, 3)),
        weight_one_grad,
        sums_one[1],
        sums_one[0],
        weight_two_grad,
        sums_two[1],
        sums_two[0],
        moment_one_new,
        moment_two_new,
        weight_norms,
        grad_norms,
    )


def solution(mesh):
    full, rows, both = P("dp", None, None, None), P("dp"), P("dp", None, None, "chan")
    weight, channel = P(None, None, "chan"), P("chan")
    return jax.shard_map(
        functools.partial(shards, mesh.shape["dp"], mesh.shape["chan"]),
        mesh=mesh,
        in_specs=(full, rows, both, weight, channel, channel, weight, channel, channel, weight, weight),
        out_specs=(both, both, weight, channel, channel, weight, channel, channel, weight, weight, P(), P()),
        check_vma=False,
    )
```

time: 833 us -> 427 us (0.51)
  matrix products: 310 us -> 0 us
  Pallas kernels: 0 us -> 170 us
  blocking collectives: 127 us -> 0 us
  local copies, waits for them, and re-layouts: 120 us -> 13.1 us
  starting transfers between devices: 0.16 us -> 54.3 us
  waiting for transfers between devices: 179 us -> 146 us
  other arithmetic: 66.2 us -> 33.7 us
  between operations: 18.3 us -> 4.21 us
    dot_general x54 -> x0, matrix products: 310 us -> none  [the longest x18 180 us: conv_back_data(): jnp.einsum('bhwd,cd->bhwc', padded[:, 2 - i:2 - i + side, 2 - j:2 - j + s...]
    pallas_call x0 -> x19, Pallas kernels: none -> 170 us  [call(): pl.pallas_call(body, out_shape=[jax.ShapeDtypeStruct(s, d) for s, d in ou...]
    ppermute x0 -> x61, waiting for transfers between devices: none -> 146 us  [swap(): return lax.ppermute(x, axis, [(i, i ^ k) for i in range(size)])]
    psum x7 -> x0, blocking collectives: 127 us -> none  [the longest x2 45.2 us: moments(): lax.psum((jnp.sum(hidden * valid_mask, axis=(0, 1, 2)), local_count), 'dp')]
    unnamed x76 -> x90, local copies, waits for them, and re-layouts: 119 us -> 8.12 us
    psum x1 -> x0, waiting for transfers between devices: 77.9 us -> none  [layer_backward(): weight_grad = lax.psum(kernel_grad(gathered, grad_h), 'dp')]
    unnamed x6 -> x0, waiting for transfers between devices: 56.8 us -> none
    ppermute x0 -> x61, starting transfers between devices: none -> 54.3 us  [swap(): return lax.ppermute(x, axis, [(i, i ^ k) for i in range(size)])]
  transfers between devices with their start and end apart: 4 -> 61, of which waited for: 4 -> 28; matrix products, arithmetic and copies ran while one was open for 17% -> 6% of each run, Pallas kernels for 0% -> 29%
where the time goes in v1:
time: 427 us; the launch traced here: 421 us
  Pallas kernels  170 us (40%)
  waiting for transfers between devices  146 us (34%)
  starting transfers between devices  54.3 us (13%)
  other arithmetic  33.7 us (8%)
  local copies, waits for them, and re-layouts  13.1 us (3%)
    pallas_call x19, Pallas kernels, call(): pl.pallas_call(body, out_shape=[jax.ShapeDtypeStruct(s, d) for s, d in ou...  170 us
    ppermute x61, waiting for transfers between devices, swap(): return lax.ppermute(x, axis, [(i, i ^ k) for i in range(size)])  146 us
    ppermute x61, starting transfers between devices, swap(): return lax.ppermute(x, axis, [(i, i ^ k) for i in range(size)])  54.3 us
  transfers between devices with their start and end apart: 61, of which 28 were waited for; matrix products, arithmetic and copies ran while one was open for 6% of the time, Pallas kernels for 29%

profile of v1, /device:TPU:0, one launch (start us, length us, event | category | flops | bytes accessed | tf_op | source)
XLA Modules:
  0.0 421.4 jit_solution(773969689715197736)
XLA Ops:
  1.3 3.5 shard_map.203
  5.5 8.9 %shard_map.204 = (f32[3,9,80,128]{3,2,1,0:T(8,128)}, f32[8,128]{1,0:T(8,128)}, bf16[3,9,80,128]{3,2,1,0:T(8,128)(2,1)}, f32[2,720,128]{2,1,0:T(8,128)}) custom-call(s32[80,128]{1,0:T(8,128)} %broadcast_in_dim.2.refs_0_.refs_1_, bf16[512,1152]{1,0:T(8,128)(2,1)} %get-tuple-element.65.refs_1_, bf16[9,9,80,512]{3,2,1,0:T(8,128)(2,1)} %bitcast.392), custom_call_target="tpu_custom_call" | custom-call | flops 3397386240 | bytes 2949120 | tf_op jit(solution)/shard_map/pallas_call | solution.py:74
  14.4 7.9 %shard_map.205 = (f32[3,9,80,128]{3,2,1,0:T(8,128)}, f32[8,128]{1,0:T(8,128)}, bf16[3,9,80,128]{3,2,1,0:T(8,128)(2,1)}, f32[2,720,128]{2,1,0:T(8,128)}) custom-call(s32[80,128]{1,0:T(8,128)} %broadcast_in_dim.2.refs_0_.refs_1_, bf16[512,1152]{1,0:T(8,128)(2,1)} %get-tuple-element.65.refs_1_, bf16[9,9,80,512]{3,2,1,0:T(8,128)(2,1)} %bitcast.393, ...), custom_call_target="tpu_custom_call" | custom-call | flops 2548039680 | bytes 2211840 | tf_op jit(solution)/shard_map/pallas_call | solution.py:74
  22.3 6.6 %shard_map.206 = (f32[3,9,80,128]{3,2,1,0:T(8,128)}, f32[8,128]{1,0:T(8,128)}, bf16[3,9,80,128]{3,2,1,0:T(8,128)(2,1)}) custom-call(s32[80,128]{1,0:T(8,128)} %broadcast_in_dim.2.refs_0_.refs_1_, bf16[512,1152]{1,0:T(8,128)(2,1)} %get-tuple-element.65.refs_1_, bf16[9,9,80,512]{3,2,1,0:T(8,128)(2,1)} %bitcast.394, f32[2,720,128]{2,1,0:T(8,128)} %get-tuple-element.68.refs_3_, ...), custom_call_target="tpu_custom_call" | custom-call | flops 1698693120 | bytes 1474560 | tf_op jit(solution)/shard_map/pallas_call | solution.py:74
  29.7 2.9 collective-permute-start.3
  35.8 2.2 collective-permute-start.4
  39.6 3.1 collective-permute-start.5
  48.4 9.8 %collective-permute-done.12.refs_4_ = bf16[3,9,80,128]{3,2,1,0:T(8,128)(2,1)S(1)} collective-permute-done((bf16[3,9,80,128]{3,2,1,0:T(8,128)(2,1)S(1)}, bf16[3,9,80,128]{3,2,1,0:T(8,128)(2,1)S(1)}, u32[]{:S(2)}, u32[]{:S(2)}) %collective-permute-start.12) | collective-permute-done | bytes 552992 | tf_op jit(solution)/shard_map/ppermute | solution.py:575
  59.7 3.5 shard_map.202
  63.2 14.9 %collective-permute-done.7 = f32[2,4,128]{2,1,0:T(4,128)S(1)} collective-permute-done((f32[2,4,128]{2,1,0:T(4,128)S(1)}, f32[2,4,128]{2,1,0:T(4,128)S(1)}, u32[]{:S(2)}, u32[]{:S(2)}) %collective-permute-start.7) | collective-permute-done | bytes 4128 | tf_op jit(solution)/shard_map/ppermute | solution.py:575
  81.3 9.4 %shard_map.207 = (f32[2,9,80,128]{3,2,1,0:T(8,128)}, f32[8,128]{1,0:T(8,128)}, bf16[3,9,80,512]{3,2,1,0:T(8,128)(2,1)}, f32[2,720,128]{2,1,0:T(8,128)}) custom-call(s32[80,128]{1,0:T(8,128)} %broadcast_in_dim.2.refs_0_.refs_1_, bf16[512,1152]{1,0:T(8,128)(2,1)} %get-tuple-element.64.refs_1_, bf16[3,9,80,128]{3,2,1,0:T(8,128)(2,1)} %get-tuple-element.73.refs_2_, ...), custom_call_target="tpu_custom_call" | custom-call | flops 2548039680 | bytes 2211840 | tf_op jit(solution)/shard_map/pallas_call | solution.py:74
  91.7 10.0 %shard_map.208 = (f32[3,9,80,128]{3,2,1,0:T(8,128)}, f32[8,128]{1,0:T(8,128)}, bf16[3,9,80,512]{3,2,1,0:T(8,128)(2,1)}, f32[2,720,128]{2,1,0:T(8,128)}) custom-call(s32[80,128]{1,0:T(8,128)} %broadcast_in_dim.2.refs_0_.refs_1_, bf16[512,1152]{1,0:T(8,128)(2,1)} %get-tuple-element.64.refs_1_, bf16[3,9,80,128]{3,2,1,0:T(8,128)(2,1)} %get-tuple-element.72.refs_2_, ...), custom_call_target="tpu_custom_call" | custom-call | flops 2548039680 | bytes 2211840 | tf_op jit(solution)/shard_map/pallas_call | solution.py:74
  102.7 10.2 %shard_map.209 = (f32[4,9,80,128]{3,2,1,0:T(8,128)}, f32[8,128]{1,0:T(8,128)}, bf16[3,9,80,512]{3,2,1,0:T(8,128)(2,1)}) custom-call(s32[80,128]{1,0:T(8,128)} %broadcast_in_dim.2.refs_0_.refs_1_, bf16[512,1152]{1,0:T(8,128)(2,1)} %get-tuple-element.64.refs_1_, bf16[3,9,80,128]{3,2,1,0:T(8,128)(2,1)} %get-tuple-element.70.refs_2_, ...), custom_call_target="tpu_custom_call" | custom-call | flops 2548039680 | bytes 2211840 | tf_op jit(solution)/shard_map/pallas_call | solution.py:74
  115.1 2.1 collective-permute-done.14
  122.9 4.1 collective-permute-done.16
  128.4 10.0 %shard_map.210 = (bf16[9,9,80,128]{3,2,1,0:T(8,128)(2,1)}, f32[2,9,80,128]{3,2,1,0:T(8,128)}, f32[3,9,80,128]{3,2,1,0:T(8,128)}, f32[4,9,80,128]{3,2,1,0:T(8,128)}, f32[8,128]{1,0:T(8,128)}) custom-call(s32[1]{0:T(128)} %bitcast.chan_ref.refs_0_, s32[80,128]{1,0:T(8,128)} %broadcast_in_dim.2.refs_0_.refs_1_, f32[4,128]{1,0:T(4,128)} %pad_maximum_fusion.13.refs_2_, ...), custom_call_target="tpu_custom_call" | custom-call | flops 82944000 | bytes 16588800 | tf_op jit(solution)/shard_map/pallas_call | solution.py:74
  140.6 2.1 collective-permute-done.20
  145.1 1.8 collective-permute-done.21
  149.6 1.8 collective-permute-done.22
  153.0 4.9 %shard_map.211 = (bf16[3,9,80,128]{3,2,1,0:T(8,128)(2,1)}, bf16[3,9,80,128]{3,2,1,0:T(8,128)(2,1)}, bf16[3,9,80,128]{3,2,1,0:T(8,128)(2,1)}) custom-call(s32[80,128]{1,0:T(8,128)} %broadcast_in_dim.2.refs_0_.refs_1_, f32[3,128]{1,0:T(4,128)} %pad_maximum_fusion.14.refs_1_, f32[2,9,80,128]{3,2,1,0:T(8,128)} %get-tuple-element.79.refs_5_.refs_2_, ...), custom_call_target="tpu_custom_call" | custom-call | flops 6635520 | bytes 8294400 | tf_op jit(solution)/shard_map/pallas_call | solution.py:74
  159.4 16.4 %shard_map.220 = f32[9,512,128]{2,1,0:T(8,128)} custom-call(s32[1]{0:T(128)} %bitcast.chan_ref.refs_0_, s32[80,128]{1,0:T(8,128)} %broadcast_in_dim.2.refs_0_.refs_1_, bf16[3,9,80,512]{3,2,1,0:T(8,128)(2,1)} %get-tuple-element.111.refs_2_, bf16[3,9,80,512]{3,2,1,0:T(8,128)(2,1)} %get-tuple-element.112.refs_3_, ...), custom_call_target="tpu_custom_call" | custom-call | flops 7644119040 | bytes 6635520 | tf_op jit(solution)/shard_map/pallas_call | solution.py:74
  175.9 1.8 select_convert_fusion
  182.7 28.7 %collective-permute-done.30.refs_4_ = bf16[3,9,80,128]{3,2,1,0:T(8,128)(2,1)S(1)} collective-permute-done((bf16[3,9,80,128]{3,2,1,0:T(8,128)(2,1)S(1)}, bf16[3,9,80,128]{3,2,1,0:T(8,128)(2,1)S(1)}, u32[]{:S(2)}, u32[]{:S(2)}) %collective-permute-start.30) | collective-permute-done | bytes 552992 | tf_op jit(solution)/shard_map/ppermute | solution.py:575
  215.7 7.7 %shard_map.212 = (f32[2,9,80,128]{3,2,1,0:T(8,128)}, f32[8,128]{1,0:T(8,128)}, f32[2,720,128]{2,1,0:T(8,128)}) custom-call(s32[80,128]{1,0:T(8,128)} %broadcast_in_dim.2.refs_0_.refs_1_, bf16[512,1152]{1,0:T(8,128)(2,1)} %pad_maximum_fusion.2.refs_1_, bf16[3,9,80,128]{3,2,1,0:T(8,128)(2,1)} %get-tuple-element.92.refs_2_.refs_5_, ...), custom_call_target="tpu_custom_call" | custom-call | flops 2548039680 | bytes 2211840 | tf_op jit(solution)/shard_map/pallas_call | solution.py:74
  224.4 17.8 %shard_map.213 = (f32[3,9,80,128]{3,2,1,0:T(8,128)}, f32[8,128]{1,0:T(8,128)}, f32[2,720,128]{2,1,0:T(8,128)}) custom-call(s32[80,128]{1,0:T(8,128)} %broadcast_in_dim.2.refs_0_.refs_1_, bf16[512,1152]{1,0:T(8,128)(2,1)} %pad_maximum_fusion.2.refs_1_, bf16[3,9,80,128]{3,2,1,0:T(8,128)(2,1)} %get-tuple-element.91.refs_2_.refs_6_, ...), custom_call_target="tpu_custom_call" | custom-call | flops 2548039680 | bytes 2211840 | tf_op jit(solution)/shard_map/pallas_call | solution.py:74
  243.2 8.8 %shard_map.214 = (f32[4,9,80,128]{3,2,1,0:T(8,128)}, f32[8,128]{1,0:T(8,128)}) custom-call(s32[80,128]{1,0:T(8,128)} %broadcast_in_dim.2.refs_0_.refs_1_, bf16[512,1152]{1,0:T(8,128)(2,1)} %pad_maximum_fusion.2.refs_1_, bf16[3,9,80,128]{3,2,1,0:T(8,128)(2,1)} %get-tuple-element.90.refs_2_.refs_7_, bf16[3,9,80,128]{3,2,1,0:T(8,128)(2,1)} %copy-done.27, ...), custom_call_target="tpu_custom_call" | custom-call | flops 2548039680 | bytes 2211840 | tf_op jit(solution)/shard_map/pallas_call | solution.py:74
  258.3 2.7 collective-permute-done.33
  261.0 2.6 collective-permute-start.34
  267.1 4.9 %shard_map.215 = (bf16[3,9,80,128]{3,2,1,0:T(8,128)(2,1)}, bf16[3,9,80,128]{3,2,1,0:T(8,128)(2,1)}, bf16[3,9,80,128]{3,2,1,0:T(8,128)(2,1)}) custom-call(s32[80,128]{1,0:T(8,128)} %broadcast_in_dim.2.refs_0_.refs_1_, f32[3,128]{1,0:T(4,128)} %pad_maximum_fusion.15.refs_1_, f32[3,9,80,128]{3,2,1,0:T(8,128)} %get-tuple-element.93.refs_7_.refs_9_.refs_2_, ...), custom_call_target="tpu_custom_call" | custom-call | flops 6635520 | bytes 8294400 | tf_op jit(solution)/shard_map/pallas_call | solution.py:74
  272.0 16.5 %shard_map.219 = f32[9,512,128]{2,1,0:T(8,128)} custom-call(s32[1]{0:T(128)} %bitcast.chan_ref.refs_0_, s32[80,128]{1,0:T(8,128)} %broadcast_in_dim.2.refs_0_.refs_1_, bf16[9,9,80,512]{3,2,1,0:T(8,128)(2,1)} %bitcast.396, bf16[3,9,80,128]{3,2,1,0:T(8,128)(2,1)} %get-tuple-element.106.refs_2_.refs_3_, ...), custom_call_target="tpu_custom_call" | custom-call | flops 7644119040 | bytes 6635520 | tf_op jit(solution)/shard_map/pallas_call | solution.py:74
  288.5 1.8 select_convert_fusion.1
  290.3 2.6 collective-permute-start.44
  300.2 2.7 collective-permute-done.44
  304.3 5.8 %collective-permute-done.54 = bf16[1152,128]{1,0:T(8,128)(2,1)S(1)} collective-permute-done((bf16[1152,128]{1,0:T(8,128)(2,1)S(1)}, bf16[1152,128]{1,0:T(8,128)(2,1)S(1)}, u32[]{:S(2)}, u32[]{:S(2)}) %collective-permute-start.54) | collective-permute-done | bytes 294944 | tf_op jit(solution)/shard_map/ppermute | solution.py:575
  312.0 18.1 %collective-permute-done.42.refs_4_ = bf16[3,9,80,128]{3,2,1,0:T(8,128)(2,1)S(1)} collective-permute-done((bf16[3,9,80,128]{3,2,1,0:T(8,128)(2,1)S(1)}, bf16[3,9,80,128]{3,2,1,0:T(8,128)(2,1)S(1)}, u32[]{:S(2)}, u32[]{:S(2)}) %collective-permute-start.42) | collective-permute-done | bytes 552992 | tf_op jit(solution)/shard_map/ppermute | solution.py:575
  331.8 9.2 %collective-permute-done.55 = bf16[2304,128]{1,0:T(8,128)(2,1)S(1)} collective-permute-done((bf16[2304,128]{1,0:T(8,128)(2,1)S(1)}, bf16[2304,128]{1,0:T(8,128)(2,1)S(1)}, u32[]{:S(2)}, u32[]{:S(2)}) %collective-permute-start.55) | collective-permute-done | bytes 589856 | tf_op jit(solution)/shard_map/ppermute | solution.py:575
  341.2 7.3 %collective-permute-done.46 = bf16[576,128]{1,0:T(8,128)(2,1)S(1)} collective-permute-done((bf16[576,128]{1,0:T(8,128)(2,1)S(1)}, bf16[576,128]{1,0:T(8,128)(2,1)S(1)}, u32[]{:S(2)}, u32[]{:S(2)}) %collective-permute-start.46) | collective-permute-done | bytes 147488 | tf_op jit(solution)/shard_map/ppermute | solution.py:575
  352.3 1.8 collective-permute-done.56
  355.5 3.5 collective-permute-done.57
  360.4 4.4 %collective-permute-done.58 = f32[4]{0:T(128)S(1)} collective-permute-done((f32[4]{0:T(128)S(1)}, f32[4]{0:T(128)S(1)}, u32[]{:S(2)}, u32[]{:S(2)}) %collective-permute-start.58) | collective-permute-done | bytes 48 | tf_op jit(solution)/shard_map/ppermute | solution.py:575
  367.5 2.0 collective-permute-done.60
  369.6 8.3 %collective-permute-done.47 = bf16[576,128]{1,0:T(8,128)(2,1)S(1)} collective-permute-done((bf16[576,128]{1,0:T(8,128)(2,1)S(1)}, bf16[576,128]{1,0:T(8,128)(2,1)S(1)}, u32[]{:S(2)}, u32[]{:S(2)}) %collective-permute-start.47) | collective-permute-done | bytes 147488 | tf_op jit(solution)/shard_map/ppermute | solution.py:575
  381.2 5.5 %collective-permute-done.48 = bf16[1152,128]{1,0:T(8,128)(2,1)S(1)} collective-permute-done((bf16[1152,128]{1,0:T(8,128)(2,1)S(1)}, bf16[1152,128]{1,0:T(8,128)(2,1)S(1)}, u32[]{:S(2)}, u32[]{:S(2)}) %collective-permute-start.48) | collective-permute-done | bytes 294944 | tf_op jit(solution)/shard_map/ppermute | solution.py:575
  386.9 1.8 collective-permute-start.49
  388.7 7.6 %shard_map.216 = (f32[9,9,80,128]{3,2,1,0:T(8,128)}, f32[2,720,128]{2,1,0:T(8,128)}) custom-call(s32[80,128]{1,0:T(8,128)} %broadcast_in_dim.2.refs_0_.refs_1_, bf16[512,1152]{1,0:T(8,128)(2,1)} %pad_maximum_fusion.1.refs_1_, bf16[3,9,80,128]{3,2,1,0:T(8,128)(2,1)} %get-tuple-element.106.refs_2_.refs_3_, bf16[3,9,80,128]{3,2,1,0:T(8,128)(2,1)} %copy-done.23, ...), custom_call_target="tpu_custom_call" | custom-call | flops 2548039680 | bytes 2211840 | tf_op jit(solution)/shard_map/pallas_call | solution.py:74
  397.1 8.0 %shard_map.217 = (f32[9,9,80,128]{3,2,1,0:T(8,128)}, f32[2,720,128]{2,1,0:T(8,128)}) custom-call(s32[80,128]{1,0:T(8,128)} %broadcast_in_dim.2.refs_0_.refs_1_, bf16[512,1152]{1,0:T(8,128)(2,1)} %pad_maximum_fusion.1.refs_1_, bf16[3,9,80,128]{3,2,1,0:T(8,128)(2,1)} %get-tuple-element.105.refs_2_.refs_4_, ...), custom_call_target="tpu_custom_call", output_to_operand_aliasing={{0}: (8, {})} | custom-call | flops 2548039680 | bytes 2211840 | tf_op jit(solution)/shard_map/pallas_call | solution.py:74
  406.2 7.5 %shard_map.218 = f32[9,9,80,128]{3,2,1,0:T(8,128)} custom-call(s32[80,128]{1,0:T(8,128)} %broadcast_in_dim.2.refs_0_.refs_1_, bf16[512,1152]{1,0:T(8,128)(2,1)} %pad_maximum_fusion.1.refs_1_, bf16[3,9,80,128]{3,2,1,0:T(8,128)(2,1)} %get-tuple-element.104.refs_2_.refs_5_, bf16[3,9,80,128]{3,2,1,0:T(8,128)(2,1)} %copy-done.9, ...), custom_call_target="tpu_custom_call", output_to_operand_aliasing={{}: (8, {})} | custom-call | flops 2548039680 | bytes 2211840 | tf_op jit(solution)/shard_map/pallas_call | solution.py:74
  415.4 5.9 %multiply_add_fusion = (f32[9,512,128]{2,1,0:T(8,128)}, f32[9,512,128]{2,1,0:T(8,128)}, f32[9,512,128]{2,1,0:T(8,128)}, f32[9,512,128]{2,1,0:T(8,128)}) fusion(f32[9,512,128]{2,1,0:T(8,128)S(1)} %copy-done, f32[9,512,128]{2,1,0:T(8,128)S(1)} %copy-done.4, f32[]{:T(128)} %bitcast.70, bf16[9,512,128]{2,1,0:T(8,128)(2,1)S(1)} %bitcast.401, ...), kind=kLoop, calls=%fused_computation.1 | loop fusion | flops 7077888 | bytes 21233672 | tf_op jit(solution)/shard_map/add | solution.py:719
  (262 shorter events, 85.9 us)
Async XLA Ops:
  29.7 4.5 %collective-permute-start.3 = (f32[3,128]{1,0:T(4,128)S(1)}, f32[3,128]{1,0:T(4,128)S(1)}, u32[]{:S(2)}, u32[]{:S(2)}) collective-permute-start(f32[3,128]{1,0:T(4,128)S(1)} %slice.215), channel_id=1, source_target_pairs={{0,4},{4,0},{8,12},{12,8},{16,20},{20,16},{24,28},{28,24},{1,5},{5... | collective-permute-start | bytes 4616 | tf_op jit(solution)/shard_map/ppermute | solution.py:575
  39.6 6.7 %collective-permute-start.5 = (f32[3,128]{1,0:T(4,128)S(1)}, f32[3,128]{1,0:T(4,128)S(1)}, u32[]{:S(2)}, u32[]{:S(2)}) collective-permute-start(f32[3,128]{1,0:T(4,128)S(1)} %pad_maximum_fusion.10), channel_id=1, source_target_pairs={{0,16},{4,20},{8,24},{12,28},{16,0},{20,4},{24,8},{28,12},{1,17},{... | collective-permute-start | bytes 4616 | tf_op jit(solution)/shard_map/ppermute | solution.py:575
  42.7 15.5 %collective-permute-start.12 = (bf16[3,9,80,128]{3,2,1,0:T(8,128)(2,1)S(1)}, bf16[3,9,80,128]{3,2,1,0:T(8,128)(2,1)S(1)}, u32[]{:S(2)}, u32[]{:S(2)}) collective-permute-start(bf16[3,9,80,128]{3,2,1,0:T(8,128)(2,1)S(1)} %copy-done.24), channel_id=1, source_target_pairs={{0,2},{1,3},{2,0},{3,1},{4,6},{5,7},{6,4},{7,5},{8,10},{9,11},{10,... | collective-permute-start | bytes 1658888 | tf_op jit(solution)/shard_map/ppermute | solution.py:575
  44.2 35.1 %collective-permute-start.11 = (bf16[3,9,80,128]{3,2,1,0:T(8,128)(2,1)S(1)}, bf16[3,9,80,128]{3,2,1,0:T(8,128)(2,1)S(1)}, u32[]{:S(2)}, u32[]{:S(2)}) collective-permute-start(bf16[3,9,80,128]{3,2,1,0:T(8,128)(2,1)S(1)} %copy-done.24), channel_id=1, source_target_pairs={{0,1},{1,0},{2,3},{3,2},{4,5},{5,4},{6,7},{7,6},{8,9},{9,8},{10,11... | collective-permute-start | bytes 1658888 | tf_op jit(solution)/shard_map/ppermute | solution.py:575
  44.2 35.2 %collective-permute-start.1 = (bf16[3,9,80,128]{3,2,1,0:T(8,128)(2,1)}, bf16[3,9,80,128]{3,2,1,0:T(8,128)(2,1)S(1)}, u32[]{:S(2)}, u32[]{:S(2)}) collective-permute-start(bf16[3,9,80,128]{3,2,1,0:T(8,128)(2,1)} %get-tuple-element.70.refs_2_), channel_id=1, source_target_pairs={{0,2},{1,3},{2,0},{3,1},{4,6},{5,7},{6,4},{7,5},{8,10},{9,11},{10,... | collective-permute-start | bytes 1658888 | tf_op jit(solution)/shard_map/ppermute | solution.py:575
  44.7 34.1 %collective-permute-start.9 = (bf16[3,9,80,128]{3,2,1,0:T(8,128)(2,1)S(1)}, bf16[3,9,80,128]{3,2,1,0:T(8,128)(2,1)S(1)}, u32[]{:S(2)}, u32[]{:S(2)}) collective-permute-start(bf16[3,9,80,128]{3,2,1,0:T(8,128)(2,1)S(1)} %copy-done.22), channel_id=1, source_target_pairs={{0,2},{1,3},{2,0},{3,1},{4,6},{5,7},{6,4},{7,5},{8,10},{9,11},{10,... | collective-permute-start | bytes 1658888 | tf_op jit(solution)/shard_map/ppermute | solution.py:575
  48.3 9.8 %collective-permute-start.6 = (f32[4,128]{1,0:T(4,128)S(1)}, f32[4,128]{1,0:T(4,128)S(1)}, u32[]{:S(2)}, u32[]{:S(2)}) collective-permute-start(f32[4,128]{1,0:T(4,128)S(1)} %get-tuple-element.178), channel_id=1, source_target_pairs={{0,1},{1,0},{2,3},{3,2},{4,5},{5,4},{6,7},{7,6},{8,9},{9,8},{10,11... | collective-permute-start | bytes 6152 | tf_op jit(solution)/shard_map/ppermute | solution.py:575
  58.1 22.3 %collective-permute-start.13 = (bf16[3,9,80,128]{3,2,1,0:T(8,128)(2,1)S(1)}, bf16[3,9,80,128]{3,2,1,0:T(8,128)(2,1)S(1)}, u32[]{:S(2)}, u32[]{:S(2)}) collective-permute-start(bf16[3,9,80,128]{3,2,1,0:T(8,128)(2,1)S(1)} %collective-permute-done.12.refs_4_), channel_id=1, source_target_pairs={{0,1},{1,0},{2,3},{3,2},{4,5},{5,4},{6,7},{7,6},{8,9},{9,8},{10,11... | collective-permute-start | bytes 1658888 | tf_op jit(solution)/shard_map/ppermute | solution.py:575
  58.2 20.0 %collective-permute-start.7 = (f32[2,4,128]{2,1,0:T(4,128)S(1)}, f32[2,4,128]{2,1,0:T(4,128)S(1)}, u32[]{:S(2)}, u32[]{:S(2)}) collective-permute-start(f32[2,4,128]{2,1,0:T(4,128)S(1)} %pad_maximum_fusion.6), channel_id=1, source_target_pairs={{0,2},{1,3},{2,0},{3,1},{4,6},{5,7},{6,4},{7,5},{8,10},{9,11},{10,... | collective-permute-start | bytes 12296 | tf_op jit(solution)/shard_map/ppermute | solution.py:575
  78.1 12.6 %collective-permute-start.8 = (bf16[3,9,80,128]{3,2,1,0:T(8,128)(2,1)S(1)}, bf16[3,9,80,128]{3,2,1,0:T(8,128)(2,1)S(1)}, u32[]{:S(2)}, u32[]{:S(2)}) collective-permute-start(bf16[3,9,80,128]{3,2,1,0:T(8,128)(2,1)S(1)} %copy-done.22), channel_id=1, source_target_pairs={{0,1},{1,0},{2,3},{3,2},{4,5},{5,4},{6,7},{7,6},{8,9},{9,8},{10,11... | collective-permute-start | bytes 1658888 | tf_op jit(solution)/shard_map/ppermute | solution.py:575
  78.8 12.0 %collective-permute-start.10 = (bf16[3,9,80,128]{3,2,1,0:T(8,128)(2,1)S(1)}, bf16[3,9,80,128]{3,2,1,0:T(8,128)(2,1)S(1)}, u32[]{:S(2)}, u32[]{:S(2)}) collective-permute-start(bf16[3,9,80,128]{3,2,1,0:T(8,128)(2,1)S(1)} %collective-permute-done.9.refs_4_), channel_id=1, source_target_pairs={{0,1},{1,0},{2,3},{3,2},{4,5},{5,4},{6,7},{7,6},{8,9},{9,8},{10,11... | collective-permute-start | bytes 1658888 | tf_op jit(solution)/shard_map/ppermute | solution.py:575
  79.3 22.4 %collective-permute-start = (bf16[3,9,80,128]{3,2,1,0:T(8,128)(2,1)S(1)}, bf16[3,9,80,128]{3,2,1,0:T(8,128)(2,1)S(1)}, u32[]{:S(2)}, u32[]{:S(2)}) collective-permute-start(bf16[3,9,80,128]{3,2,1,0:T(8,128)(2,1)S(1)} %copy-done.20), channel_id=1, source_target_pairs={{0,1},{1,0},{2,3},{3,2},{4,5},{5,4},{6,7},{7,6},{8,9},{9,8},{10,11... | collective-permute-start | bytes 1658888 | tf_op jit(solution)/shard_map/ppermute | solution.py:575
  79.4 22.3 %collective-permute-start.2 = (bf16[3,9,80,128]{3,2,1,0:T(8,128)(2,1)S(1)}, bf16[3,9,80,128]{3,2,1,0:T(8,128)(2,1)S(1)}, u32[]{:S(2)}, u32[]{:S(2)}) collective-permute-start(bf16[3,9,80,128]{3,2,1,0:T(8,128)(2,1)S(1)} %collective-permute-done.1.refs_4_), channel_id=1, source_target_pairs={{0,1},{1,0},{2,3},{3,2},{4,5},{5,4},{6,7},{7,6},{8,9},{9,8},{10,11... | collective-permute-start | bytes 1658888 | tf_op jit(solution)/shard_map/ppermute | solution.py:575
  122.4 4.5 %collective-permute-start.16 = (f32[3,128]{1,0:T(4,128)S(1)}, f32[3,128]{1,0:T(4,128)S(1)}, u32[]{:S(2)}, u32[]{:S(2)}) collective-permute-start(f32[3,128]{1,0:T(4,128)S(1)} %pad_maximum_fusion.12), channel_id=1, source_target_pairs={{0,16},{4,20},{8,24},{12,28},{16,0},{20,4},{24,8},{28,12},{1,17},{... | collective-permute-start | bytes 4616 | tf_op jit(solution)/shard_map/ppermute | solution.py:575
  147.0 4.5 %collective-permute-start.22 = (f32[2,128]{1,0:T(2,128)S(1)}, f32[2,128]{1,0:T(2,128)S(1)}, u32[]{:S(2)}, u32[]{:S(2)}) collective-permute-start(f32[2,128]{1,0:T(2,128)S(1)} %add.386), channel_id=1, source_target_pairs={{0,16},{4,20},{8,24},{12,28},{16,0},{20,4},{24,8},{28,12},{1,17},{... | collective-permute-start | bytes 3080 | tf_op jit(solution)/shard_map/ppermute | solution.py:575
  147.4 30.3 %collective-permute-start.17 = (bf16[2,128,1152]{2,1,0:T(8,128)(2,1)S(1)}, bf16[2,128,1152]{2,1,0:T(8,128)(2,1)S(1)}, u32[]{:S(2)}, u32[]{:S(2)}) collective-permute-start(bf16[2,128,1152]{2,1,0:T(8,128)(2,1)S(1)} %get-tuple-element.159), channel_id=1, source_target_pairs={{0,1},{1,0},{2,3},{3,2},{4,5},{5,4},{6,7},{7,6},{8,9},{9,8},{10,11... | collective-permute-start | bytes 1769480 | tf_op jit(solution)/shard_map/ppermute | solution.py:575
  147.5 30.8 %collective-permute-start.19 = (bf16[2,128,1152]{2,1,0:T(8,128)(2,1)S(1)}, bf16[2,128,1152]{2,1,0:T(8,128)(2,1)S(1)}, u32[]{:S(2)}, u32[]{:S(2)}) collective-permute-start(bf16[2,128,1152]{2,1,0:T(8,128)(2,1)S(1)} %get-tuple-element.160), channel_id=1, source_target_pairs={{0,3},{1,2},{2,1},{3,0},{4,7},{5,6},{6,5},{7,4},{8,11},{9,10},{10,... | collective-permute-start | bytes 1769480 | tf_op jit(solution)/shard_map/ppermute | solution.py:575
  149.1 30.9 %collective-permute-start.18 = (bf16[2,128,1152]{2,1,0:T(8,128)(2,1)S(1)}, bf16[2,128,1152]{2,1,0:T(8,128)(2,1)S(1)}, u32[]{:S(2)}, u32[]{:S(2)}) collective-permute-start(bf16[2,128,1152]{2,1,0:T(8,128)(2,1)S(1)} %get-tuple-element.161), channel_id=1, source_target_pairs={{0,2},{1,3},{2,0},{3,1},{4,6},{5,7},{6,4},{7,5},{8,10},{9,11},{10,... | collective-permute-start | bytes 1769480 | tf_op jit(solution)/shard_map/ppermute | solution.py:575
  157.9 54.3 %collective-permute-start.24 = (bf16[3,9,80,128]{3,2,1,0:T(8,128)(2,1)}, bf16[3,9,80,128]{3,2,1,0:T(8,128)(2,1)S(1)}, u32[]{:S(2)}, u32[]{:S(2)}) collective-permute-start(bf16[3,9,80,128]{3,2,1,0:T(8,128)(2,1)} %get-tuple-element.90.refs_2_.refs_7_), channel_id=1, source_target_pairs={{0,2},{1,3},{2,0},{3,1},{4,6},{5,7},{6,4},{7,5},{8,10},{9,11},{10,... | collective-permute-start | bytes 1658888 | tf_op jit(solution)/shard_map/ppermute | solution.py:575
  159.4 82.7 %collective-permute-start.23 = (bf16[3,9,80,128]{3,2,1,0:T(8,128)(2,1)}, bf16[3,9,80,128]{3,2,1,0:T(8,128)(2,1)S(1)}, u32[]{:S(2)}, u32[]{:S(2)}) collective-permute-start(bf16[3,9,80,128]{3,2,1,0:T(8,128)(2,1)} %get-tuple-element.90.refs_2_.refs_7_), channel_id=1, source_target_pairs={{0,1},{1,0},{2,3},{3,2},{4,5},{5,4},{6,7},{7,6},{8,9},{9,8},{10,11... | collective-permute-start | bytes 1658888 | tf_op jit(solution)/shard_map/ppermute | solution.py:575
  177.7 34.6 %collective-permute-start.27 = (bf16[3,9,80,128]{3,2,1,0:T(8,128)(2,1)}, bf16[3,9,80,128]{3,2,1,0:T(8,128)(2,1)S(1)}, u32[]{:S(2)}, u32[]{:S(2)}) collective-permute-start(bf16[3,9,80,128]{3,2,1,0:T(8,128)(2,1)} %get-tuple-element.91.refs_2_.refs_6_), channel_id=1, source_target_pairs={{0,2},{1,3},{2,0},{3,1},{4,6},{5,7},{6,4},{7,5},{8,10},{9,11},{10,... | collective-permute-start | bytes 1658888 | tf_op jit(solution)/shard_map/ppermute | solution.py:575
  178.3 33.0 %collective-permute-start.30 = (bf16[3,9,80,128]{3,2,1,0:T(8,128)(2,1)S(1)}, bf16[3,9,80,128]{3,2,1,0:T(8,128)(2,1)S(1)}, u32[]{:S(2)}, u32[]{:S(2)}) collective-permute-start(bf16[3,9,80,128]{3,2,1,0:T(8,128)(2,1)S(1)} %copy-done.31), channel_id=1, source_target_pairs={{0,2},{1,3},{2,0},{3,1},{4,6},{5,7},{6,4},{7,5},{8,10},{9,11},{10,... | collective-permute-start | bytes 1658888 | tf_op jit(solution)/shard_map/ppermute | solution.py:575
  180.0 31.4 %collective-permute-start.50 = (bf16[2304,128]{1,0:T(8,128)(2,1)S(1)}, bf16[2304,128]{1,0:T(8,128)(2,1)S(1)}, u32[]{:S(2)}, u32[]{:S(2)}) collective-permute-start(bf16[2304,128]{1,0:T(8,128)(2,1)S(1)} %select_convert_fusion), channel_id=1, source_target_pairs={{0,4},{4,0},{8,12},{12,8},{16,20},{20,16},{24,28},{28,24},{1,5},{5... | collective-permute-start | bytes 1769480 | tf_op jit(solution)/shard_map/ppermute | solution.py:575
  212.2 11.1 %collective-permute-start.26 = (bf16[3,9,80,128]{3,2,1,0:T(8,128)(2,1)}, bf16[3,9,80,128]{3,2,1,0:T(8,128)(2,1)S(1)}, u32[]{:S(2)}, u32[]{:S(2)}) collective-permute-start(bf16[3,9,80,128]{3,2,1,0:T(8,128)(2,1)} %get-tuple-element.91.refs_2_.refs_6_), channel_id=1, source_target_pairs={{0,1},{1,0},{2,3},{3,2},{4,5},{5,4},{6,7},{7,6},{8,9},{9,8},{10,11... | collective-permute-start | bytes 1658888 | tf_op jit(solution)/shard_map/ppermute | solution.py:575
  212.2 29.9 %collective-permute-start.25 = (bf16[3,9,80,128]{3,2,1,0:T(8,128)(2,1)S(1)}, bf16[3,9,80,128]{3,2,1,0:T(8,128)(2,1)S(1)}, u32[]{:S(2)}, u32[]{:S(2)}) collective-permute-start(bf16[3,9,80,128]{3,2,1,0:T(8,128)(2,1)S(1)} %collective-permute-done.24.refs_4_), channel_id=1, source_target_pairs={{0,1},{1,0},{2,3},{3,2},{4,5},{5,4},{6,7},{7,6},{8,9},{9,8},{10,11... | collective-permute-start | bytes 1658888 | tf_op jit(solution)/shard_map/ppermute | solution.py:575
  213.3 10.1 %collective-permute-start.28 = (bf16[3,9,80,128]{3,2,1,0:T(8,128)(2,1)S(1)}, bf16[3,9,80,128]{3,2,1,0:T(8,128)(2,1)S(1)}, u32[]{:S(2)}, u32[]{:S(2)}) collective-permute-start(bf16[3,9,80,128]{3,2,1,0:T(8,128)(2,1)S(1)} %collective-permute-done.27.refs_4_), channel_id=1, source_target_pairs={{0,1},{1,0},{2,3},{3,2},{4,5},{5,4},{6,7},{7,6},{8,9},{9,8},{10,11... | collective-permute-start | bytes 1658888 | tf_op jit(solution)/shard_map/ppermute | solution.py:575
  214.1 44.1 %collective-permute-start.51 = (bf16[1152,128]{1,0:T(8,128)(2,1)S(1)}, bf16[1152,128]{1,0:T(8,128)(2,1)S(1)}, u32[]{:S(2)}, u32[]{:S(2)}) collective-permute-start(bf16[1152,128]{1,0:T(8,128)(2,1)S(1)} %select_convert_fusion.2), channel_id=1, source_target_pairs={{0,8},{4,12},{8,0},{12,4},{16,24},{20,28},{24,16},{28,20},{1,9},{5... | collective-permute-start | bytes 884744 | tf_op jit(solution)/shard_map/ppermute | solution.py:575
  261.0 4.5 %collective-permute-start.34 = (f32[2,128]{1,0:T(2,128)S(1)}, f32[2,128]{1,0:T(2,128)S(1)}, u32[]{:S(2)}, u32[]{:S(2)}) collective-permute-start(f32[2,128]{1,0:T(2,128)S(1)} %add.395), channel_id=1, source_target_pairs={{0,16},{4,20},{8,24},{12,28},{16,0},{20,4},{24,8},{28,12},{1,17},{... | collective-permute-start | bytes 3080 | tf_op jit(solution)/shard_map/ppermute | solution.py:575
  263.5 29.4 %collective-permute-start.52 = (bf16[576,128]{1,0:T(8,128)(2,1)S(1)}, bf16[576,128]{1,0:T(8,128)(2,1)S(1)}, u32[]{:S(2)}, u32[]{:S(2)}) collective-permute-start(bf16[576,128]{1,0:T(8,128)(2,1)S(1)} %select_convert_fusion.4), channel_id=1, source_target_pairs={{0,16},{4,20},{8,24},{12,28},{16,0},{20,4},{24,8},{28,12},{1,17},{... | collective-permute-start | bytes 442376 | tf_op jit(solution)/shard_map/ppermute | solution.py:575
  290.3 12.6 %collective-permute-start.44 = (bf16[2304,128]{1,0:T(8,128)(2,1)S(1)}, bf16[2304,128]{1,0:T(8,128)(2,1)S(1)}, u32[]{:S(2)}, u32[]{:S(2)}) collective-permute-start(bf16[2304,128]{1,0:T(8,128)(2,1)S(1)} %select_convert_fusion.1), channel_id=1, source_target_pairs={{0,4},{4,0},{8,12},{12,8},{16,20},{20,16},{24,28},{28,24},{1,5},{5... | collective-permute-start | bytes 1769480 | tf_op jit(solution)/shard_map/ppermute | solution.py:575
  293.6 6.4 %collective-permute-start.53 = (bf16[576,128]{1,0:T(8,128)(2,1)S(1)}, bf16[576,128]{1,0:T(8,128)(2,1)S(1)}, u32[]{:S(2)}, u32[]{:S(2)}) collective-permute-start(bf16[576,128]{1,0:T(8,128)(2,1)S(1)} %get-tuple-element.162), channel_id=1, source_target_pairs={{0,16},{4,20},{8,24},{12,28},{16,0},{20,4},{24,8},{28,12},{1,17},{... | collective-permute-start | bytes 442376 | tf_op jit(solution)/shard_map/ppermute | solution.py:575
  295.8 84.7 %collective-permute-start.36 = (bf16[3,9,80,128]{3,2,1,0:T(8,128)(2,1)S(1)}, bf16[3,9,80,128]{3,2,1,0:T(8,128)(2,1)S(1)}, u32[]{:S(2)}, u32[]{:S(2)}) collective-permute-start(bf16[3,9,80,128]{3,2,1,0:T(8,128)(2,1)S(1)} %copy-done.7), channel_id=1, source_target_pairs={{0,2},{1,3},{2,0},{3,1},{4,6},{5,7},{6,4},{7,5},{8,10},{9,11},{10,... | collective-permute-start | bytes 1658888 | tf_op jit(solution)/shard_map/ppermute | solution.py:575
  297.3 83.3 %collective-permute-start.39 = (bf16[3,9,80,128]{3,2,1,0:T(8,128)(2,1)S(1)}, bf16[3,9,80,128]{3,2,1,0:T(8,128)(2,1)S(1)}, u32[]{:S(2)}, u32[]{:S(2)}) collective-permute-start(bf16[3,9,80,128]{3,2,1,0:T(8,128)(2,1)S(1)} %copy-done.17), channel_id=1, source_target_pairs={{0,2},{1,3},{2,0},{3,1},{4,6},{5,7},{6,4},{7,5},{8,10},{9,11},{10,... | collective-permute-start | bytes 1658888 | tf_op jit(solution)/shard_map/ppermute | solution.py:575
  297.8 32.3 %collective-permute-start.42 = (bf16[3,9,80,128]{3,2,1,0:T(8,128)(2,1)S(1)}, bf16[3,9,80,128]{3,2,1,0:T(8,128)(2,1)S(1)}, u32[]{:S(2)}, u32[]{:S(2)}) collective-permute-start(bf16[3,9,80,128]{3,2,1,0:T(8,128)(2,1)S(1)} %copy-done.18), channel_id=1, source_target_pairs={{0,2},{1,3},{2,0},{3,1},{4,6},{5,7},{6,4},{7,5},{8,10},{9,11},{10,... | collective-permute-start | bytes 1658888 | tf_op jit(solution)/shard_map/ppermute | solution.py:575
  300.1 81.0 %collective-permute-start.41 = (bf16[3,9,80,128]{3,2,1,0:T(8,128)(2,1)S(1)}, bf16[3,9,80,128]{3,2,1,0:T(8,128)(2,1)S(1)}, u32[]{:S(2)}, u32[]{:S(2)}) collective-permute-start(bf16[3,9,80,128]{3,2,1,0:T(8,128)(2,1)S(1)} %copy-done.18), channel_id=1, source_target_pairs={{0,1},{1,0},{2,3},{3,2},{4,5},{5,4},{6,7},{7,6},{8,9},{9,8},{10,11... | collective-permute-start | bytes 1658888 | tf_op jit(solution)/shard_map/ppermute | solution.py:575
  302.9 7.2 %collective-permute-start.54 = (bf16[1152,128]{1,0:T(8,128)(2,1)S(1)}, bf16[1152,128]{1,0:T(8,128)(2,1)S(1)}, u32[]{:S(2)}, u32[]{:S(2)}) collective-permute-start(bf16[1152,128]{1,0:T(8,128)(2,1)S(1)} %maximum_select_fusion.5), channel_id=1, source_target_pairs={{0,8},{4,12},{8,0},{12,4},{16,24},{20,28},{24,16},{28,20},{1,9},{5... | collective-permute-start | bytes 884744 | tf_op jit(solution)/shard_map/ppermute | solution.py:575
  310.1 21.6 %collective-permute-start.45 = (bf16[1152,128]{1,0:T(8,128)(2,1)S(1)}, bf16[1152,128]{1,0:T(8,128)(2,1)S(1)}, u32[]{:S(2)}, u32[]{:S(2)}) collective-permute-start(bf16[1152,128]{1,0:T(8,128)(2,1)S(1)} %select_convert_fusion.3), channel_id=1, source_target_pairs={{0,8},{4,12},{8,0},{12,4},{16,24},{20,28},{24,16},{28,20},{1,9},{5... | collective-permute-start | bytes 884744 | tf_op jit(solution)/shard_map/ppermute | solution.py:575
  330.1 10.8 %collective-permute-start.55 = (bf16[2304,128]{1,0:T(8,128)(2,1)S(1)}, bf16[2304,128]{1,0:T(8,128)(2,1)S(1)}, u32[]{:S(2)}, u32[]{:S(2)}) collective-permute-start(bf16[2304,128]{1,0:T(8,128)(2,1)S(1)} %maximum_select_fusion.3), channel_id=1, source_target_pairs={{0,4},{4,0},{8,12},{12,8},{16,20},{20,16},{24,28},{28,24},{1,5},{5... | collective-permute-start | bytes 1769480 | tf_op jit(solution)/shard_map/ppermute | solution.py:575
  331.6 55.3 %collective-permute-start.43 = (bf16[3,9,80,128]{3,2,1,0:T(8,128)(2,1)S(1)}, bf16[3,9,80,128]{3,2,1,0:T(8,128)(2,1)}, u32[]{:S(2)}, u32[]{:S(2)}) collective-permute-start(bf16[3,9,80,128]{3,2,1,0:T(8,128)(2,1)S(1)} %collective-permute-done.42.refs_4_), channel_id=1, source_target_pairs={{0,1},{1,0},{2,3},{3,2},{4,5},{5,4},{6,7},{7,6},{8,9},{9,8},{10,11... | collective-permute-start | bytes 1658888 | tf_op jit(solution)/shard_map/ppermute | solution.py:575
  340.9 7.6 %collective-permute-start.46 = (bf16[576,128]{1,0:T(8,128)(2,1)S(1)}, bf16[576,128]{1,0:T(8,128)(2,1)S(1)}, u32[]{:S(2)}, u32[]{:S(2)}) collective-permute-start(bf16[576,128]{1,0:T(8,128)(2,1)S(1)} %select_convert_fusion.5), channel_id=1, source_target_pairs={{0,16},{4,20},{8,24},{12,28},{16,0},{20,4},{24,8},{28,12},{1,17},{... | collective-permute-start | bytes 442376 | tf_op jit(solution)/shard_map/ppermute | solution.py:575
  360.4 4.4 %collective-permute-start.58 = (f32[4]{0:T(128)S(1)}, f32[4]{0:T(128)S(1)}, u32[]{:S(2)}, u32[]{:S(2)}) collective-permute-start(f32[4]{0:T(128)S(1)} %fusion.44), channel_id=1, source_target_pairs={{0,16},{4,20},{8,24},{12,28},{16,0},{20,4},{24,8},{28,12},{1,17},{... | collective-permute-start | bytes 56 | tf_op jit(solution)/shard_map/ppermute | solution.py:575
  369.5 8.3 %collective-permute-start.47 = (bf16[576,128]{1,0:T(8,128)(2,1)S(1)}, bf16[576,128]{1,0:T(8,128)(2,1)S(1)}, u32[]{:S(2)}, u32[]{:S(2)}) collective-permute-start(bf16[576,128]{1,0:T(8,128)(2,1)S(1)} %get-tuple-element.164), channel_id=1, source_target_pairs={{0,16},{4,20},{8,24},{12,28},{16,0},{20,4},{24,8},{28,12},{1,17},{... | collective-permute-start | bytes 442376 | tf_op jit(solution)/shard_map/ppermute | solution.py:575
  377.9 8.8 %collective-permute-start.48 = (bf16[1152,128]{1,0:T(8,128)(2,1)S(1)}, bf16[1152,128]{1,0:T(8,128)(2,1)S(1)}, u32[]{:S(2)}, u32[]{:S(2)}) collective-permute-start(bf16[1152,128]{1,0:T(8,128)(2,1)S(1)} %maximum_select_fusion.4), channel_id=1, source_target_pairs={{0,8},{4,12},{8,0},{12,4},{16,24},{20,28},{24,16},{28,20},{1,9},{5... | collective-permute-start | bytes 884744 | tf_op jit(solution)/shard_map/ppermute | solution.py:575
  380.5 24.7 %collective-permute-start.35 = (bf16[3,9,80,128]{3,2,1,0:T(8,128)(2,1)S(1)}, bf16[3,9,80,128]{3,2,1,0:T(8,128)(2,1)S(1)}, u32[]{:S(2)}, u32[]{:S(2)}) collective-permute-start(bf16[3,9,80,128]{3,2,1,0:T(8,128)(2,1)S(1)} %copy-done.7), channel_id=1, source_target_pairs={{0,1},{1,0},{2,3},{3,2},{4,5},{5,4},{6,7},{7,6},{8,9},{9,8},{10,11... | collective-permute-start | bytes 1658888 | tf_op jit(solution)/shard_map/ppermute | solution.py:575
  380.6 15.7 %collective-permute-start.38 = (bf16[3,9,80,128]{3,2,1,0:T(8,128)(2,1)S(1)}, bf16[3,9,80,128]{3,2,1,0:T(8,128)(2,1)}, u32[]{:S(2)}, u32[]{:S(2)}) collective-permute-start(bf16[3,9,80,128]{3,2,1,0:T(8,128)(2,1)S(1)} %copy-done.17), channel_id=1, source_target_pairs={{0,1},{1,0},{2,3},{3,2},{4,5},{5,4},{6,7},{7,6},{8,9},{9,8},{10,11... | collective-permute-start | bytes 1658888 | tf_op jit(solution)/shard_map/ppermute | solution.py:575
  381.1 24.1 %collective-permute-start.37 = (bf16[3,9,80,128]{3,2,1,0:T(8,128)(2,1)S(1)}, bf16[3,9,80,128]{3,2,1,0:T(8,128)(2,1)S(1)}, u32[]{:S(2)}, u32[]{:S(2)}) collective-permute-start(bf16[3,9,80,128]{3,2,1,0:T(8,128)(2,1)S(1)} %collective-permute-done.36.refs_4_), channel_id=1, source_target_pairs={{0,1},{1,0},{2,3},{3,2},{4,5},{5,4},{6,7},{7,6},{8,9},{9,8},{10,11... | collective-permute-start | bytes 1658888 | tf_op jit(solution)/shard_map/ppermute | solution.py:575
  386.7 9.6 %collective-permute-start.40 = (bf16[3,9,80,128]{3,2,1,0:T(8,128)(2,1)S(1)}, bf16[3,9,80,128]{3,2,1,0:T(8,128)(2,1)S(1)}, u32[]{:S(2)}, u32[]{:S(2)}) collective-permute-start(bf16[3,9,80,128]{3,2,1,0:T(8,128)(2,1)S(1)} %collective-permute-done.39.refs_4_), channel_id=1, source_target_pairs={{0,1},{1,0},{2,3},{3,2},{4,5},{5,4},{6,7},{7,6},{8,9},{9,8},{10,11... | collective-permute-start | bytes 1658888 | tf_op jit(solution)/shard_map/ppermute | solution.py:575
  386.9 26.8 %collective-permute-start.49 = (bf16[2304,128]{1,0:T(8,128)(2,1)S(1)}, bf16[2304,128]{1,0:T(8,128)(2,1)S(1)}, u32[]{:S(2)}, u32[]{:S(2)}) collective-permute-start(bf16[2304,128]{1,0:T(8,128)(2,1)S(1)} %maximum_select_fusion.2), channel_id=1, source_target_pairs={{0,4},{4,0},{8,12},{12,8},{16,20},{20,16},{24,28},{28,24},{1,5},{5... | collective-permute-start | bytes 1769480 | tf_op jit(solution)/shard_map/ppermute | solution.py:575
  (58 other events, 471.0 us)
